TPU v7x, 128 devices: a whole 4x4x4 slice. The times are simulated.
128 devices in a mesh: dp: 16 (over y_lo, x, core), tensor: 8 (over z, y_hi).
Axes of the slice: x: 4, y: 4 (y_hi: 2, y_lo: 2; y = y_hi * 2 + y_lo), z: 4, core: 2. Of those that a mesh axis runs over, the one named last changes fastest.
Arguments:
- x_in: bfloat16 [32768, 1536], P(('dp', 'tensor')), may hold values from -6 to 6
- cotangent: bfloat16 [32768, 1536], P(('dp', 'tensor')), may hold values from -6 to 6
- seq_lengths: int32 [16, 2], P('dp'), may hold values from 0 to 2048, as said below
- in_gain: float32 [1536], replicated, may hold values from 0.1 to 1.9
- w_z: bfloat16 [1536, 3072], P('dp', 'tensor'), may hold values from -0.15625 to 0.15625
- w_x: bfloat16 [1536, 3072], P('dp', 'tensor'), may hold values from -0.15625 to 0.15625
- w_dt: bfloat16 [1536, 48], P('dp', 'tensor'), may hold values from -0.15625 to 0.15625
- w_bc: bfloat16 [1536, 256], P('dp'), may hold values from -0.15625 to 0.15625
- conv_wx: float32 [4, 3072], P(None, 'tensor'), may hold values from -3 to 3
- conv_bx: float32 [3072], P('tensor'), may hold values from -3 to 3
- conv_wbc: float32 [4, 256], replicated, may hold values from -3 to 3
- conv_bbc: float32 [256], replicated, may hold values from -3 to 3
- dt_bias: float32 [48], P('tensor'), may hold values from -6 to -2
- a_log: float32 [48], P('tensor'), may hold values from 0 to 2.77
- d_skip: float32 [48], P('tensor'), may hold values from 0.5 to 1.5
- gnorm_gain: float32 [3072], P('tensor'), may hold values from 0.1 to 1.9
- w_out: bfloat16 [1536, 3072], P('dp', 'tensor'), may hold values from -0.109375 to 0.109375
Outputs:
- output: bfloat16 [32768, 1536], P(('dp', 'tensor'))
- x_grad: float32 [32768, 1536], P(('dp', 'tensor'))
- in_gain_grad: float32 [1536], P(('dp', 'tensor'))
- w_z_grad: float32 [1536, 3072], P('dp', 'tensor')
- w_x_grad: float32 [1536, 3072], P('dp', 'tensor')
- w_dt_grad: float32 [1536, 48], P('dp', 'tensor')
- w_bc_grad: float32 [1536, 256], P('dp')
- conv_wx_grad: float32 [4, 3072], P(None, 'tensor')
- conv_bx_grad: float32 [3072], P('tensor')
- conv_wbc_grad: float32 [4, 256], replicated
- conv_bbc_grad: float32 [256], replicated
- dt_bias_grad: float32 [48], P('tensor')
- a_log_grad: float32 [48], P('tensor')
- d_skip_grad: float32 [48], P('tensor')
- gnorm_gain_grad: float32 [3072], P('tensor')
- w_out_grad: float32 [1536, 3072], P('dp', 'tensor')
Inputs may be any that keep to these rules, and one draw needn't show every extreme that they name: `seq_lengths`: row g lists the lengths of group g's sequences; a 0 is followed only by 0s, the first entry is positive, every positive length is 1024 or more, and the lengths rounded up to multiples of 256 sum to at most 2048. Some group holds one sequence of exactly 2048 tokens.
All inputs are finite; a program needn't handle non-finite values.
Results may differ from a plain program's by a relative error of at most 0.012.
Values may be sent and summed in bfloat16 or wider, within the bound.
No kernel may reach another device: no remote copies, remote signals or barrier semaphores. Data moves between devices by JAX's collectives and lax.ppermute only.
A program may use at most 192 MiB of HBM per device.

v0:
```python
import jax
import jax.numpy as jnp
from jax import lax
from jax.sharding import PartitionSpec as P

CH = 256
DI = 3072


EPS = 1e-05
HIGH = lax.Precision.HIGHEST


def exact_dot(left, right):
    return jnp.dot(left, right, precision=HIGH, preferred_element_type=jnp.float32)


def contract_rows(left, right):
    return lax.dot_general(
        left, right, (((0,), (0,)), ((), ())), preferred_element_type=jnp.float32
    )


def contract_cols(left, right):
    return lax.dot_general(
        left, right, (((1,), (1,)), ((), ())), preferred_element_type=jnp.float32
    )


def layout(lengths, group_len, stretch):
    stretch_count = (lengths + stretch - 1) // stretch
    padded_span = stretch_count * stretch
    offsets = jnp.cumsum(padded_span) - padded_span
    token_place = jnp.arange(group_len, dtype=jnp.int32)
    inside = (token_place[:, None] >= offsets[None, :]) & (
        token_place[:, None] < (offsets + padded_span)[None, :]
    )
    position = jnp.sum(jnp.where(inside, token_place[:, None] - offsets[None, :], 0), axis=1)
    within = (token_place[:, None] >= offsets[None, :]) & (
        token_place[:, None] < (offsets + lengths)[None, :]
    )
    live_mask = jnp.sum(within.astype(jnp.float32), axis=1)
    keep_state = (position[::stretch] > 0).astype(jnp.float32)
    return (position, live_mask, keep_state)


def conv_silu(values, taps, offset, position):
    width = taps.shape[0]
    padded = jnp.pad(values, ((width - 1, 0), (0, 0)))
    running = offset + jnp.zeros_like(values)
    for j in range(width):
        shifted = padded[width - 1 - j : width - 1 - j + values.shape[0]]
        running = running + taps[width - 1 - j] * shifted * (position >= j)[:, None].astype(
            jnp.float32
        )
    return jax.nn.silu(running)


def state_space(inner, states, step_pre, dt_bias, a_log, d_skip, keep_state):
    group_len = inner.shape[0]
    heads = step_pre.shape[1]
    hsize = inner.shape[1] // heads
    nstate = states.shape[1] // 2
    count = group_len // CH
    step_size = jax.nn.softplus(step_pre + dt_bias)
    decay_rate = step_size * -jnp.exp(a_log)
    x_blocks = inner.reshape(count, CH, heads, hsize)
    b_blocks = states[:, :nstate].reshape(count, CH, nstate)
    c_blocks = states[:, nstate:].reshape(count, CH, nstate)
    s_blocks = step_size.reshape(count, CH, heads)
    r_blocks = decay_rate.reshape(count, CH, heads)
    lower = jnp.arange(CH)[:, None] >= jnp.arange(CH)[None, :]

    def advance(carried, pieces):
        xc, bc, cc, sc, rc, kc = pieces
        cumulate = jnp.cumsum(rc, axis=0)
        carried = carried * kc
        scores = exact_dot(cc, bc.T)
        diff = cumulate.T[:, :, None] - cumulate.T[:, None, :]
        decay_term = jnp.exp(jnp.where(lower[None], diff, -1e30))
        mixing = scores[None] * decay_term * sc.T[:, None, :]
        diagonal = jnp.einsum("hij,jhp->ihp", mixing, xc, precision=HIGH)
        carried_part = (
            jnp.einsum("in,hpn->ihp", cc, carried, precision=HIGH) * jnp.exp(cumulate)[:, :, None]
        )
        weights = jnp.exp(cumulate[-1][None, :] - cumulate) * sc
        updated = carried * jnp.exp(cumulate[-1])[:, None, None] + jnp.einsum(
            "jh,jn,jhp->hpn", weights, bc, xc, precision=HIGH
        )
        return (updated, diagonal + carried_part)

    start = jnp.zeros((heads, hsize, nstate), jnp.float32)
    _, blocks = lax.scan(
        jax.checkpoint(advance),
        start,
        (x_blocks, b_blocks, c_blocks, s_blocks, r_blocks, keep_state),
    )
    return blocks.reshape(group_len, heads * hsize) + inner * jnp.repeat(d_skip, hsize)


def rounded(value):
    return lax.optimization_barrier(value.astype(jnp.bfloat16)).astype(jnp.float32)


def local(
    x_in,
    cotangent,
    seq_lengths,
    in_gain,
    w_z,
    w_x,
    w_dt,
    w_bc,
    conv_wx,
    conv_bx,
    conv_wbc,
    conv_bbc,
    dt_bias,
    a_log,
    d_skip,
    gnorm_gain,
    w_out,
):
    row_count = x_in.shape[0]
    model_width = x_in.shape[1]
    group_len = row_count * lax.axis_size("tensor")
    start_row = lax.axis_index("tensor") * row_count
    position, live_mask, keep_state = layout(seq_lengths[0], group_len, CH)
    own_live = lax.dynamic_slice_in_dim(live_mask, start_row, row_count, 0)
    resid = x_in.astype(jnp.float32)
    inverse = lax.rsqrt(jnp.mean(resid * resid, axis=-1, keepdims=True) + EPS)
    normed = (resid * inverse * in_gain).astype(jnp.bfloat16)
    full_z, full_x, full_dt, full_bc, full_out = (
        lax.all_gather(w_z, "dp", axis=0, tiled=True),
        lax.all_gather(w_x, "dp", axis=0, tiled=True),
        lax.all_gather(w_dt, "dp", axis=0, tiled=True),
        lax.all_gather(w_bc, "dp", axis=0, tiled=True),
        lax.all_gather(w_out, "dp", axis=0, tiled=True),
    )
    tokens = lax.all_gather(normed, "tensor", axis=0, tiled=True)
    gate = jnp.dot(tokens, full_z, preferred_element_type=jnp.float32)
    inner_pre = jnp.dot(tokens, full_x, preferred_element_type=jnp.float32)
    state_pre = jnp.dot(tokens, full_bc, preferred_element_type=jnp.float32)
    step_pre = jnp.dot(tokens, full_dt, preferred_element_type=jnp.float32)

    def convolve(values, taps, offset):
        return conv_silu(values, taps, offset, position)

    inner_act, inner_pullback = jax.vjp(convolve, inner_pre, conv_wx, conv_bx)
    state_act, state_pullback = jax.vjp(convolve, state_pre, conv_wbc, conv_bbc)

    def mixer(inner, states, steps, bias, decay, skip):
        return state_space(inner, states, steps, bias, decay, skip, keep_state)

    mixed, mixer_pullback = jax.vjp(
        mixer, rounded(inner_act), rounded(state_act), step_pre, dt_bias, a_log, d_skip
    )
    silu_gate = jax.nn.silu(gate)
    gated = mixed * silu_gate
    square_sum = lax.psum(jnp.sum(gated * gated, axis=-1), "tensor")
    scale = lax.rsqrt(square_sum / DI + EPS)[:, None]
    hidden = (gated * scale * gnorm_gain).astype(jnp.bfloat16)
    branch = lax.psum_scatter(
        contract_cols(hidden, full_out).astype(jnp.bfloat16),
        "tensor",
        scatter_dimension=0,
        tiled=True,
    ).astype(jnp.float32)
    output = (resid + own_live[:, None] * branch).astype(jnp.bfloat16)
    back_z, back_x, back_dt, back_bc, back_out = (
        lax.all_gather(w_z, "dp", axis=0, tiled=True),
        lax.all_gather(w_x, "dp", axis=0, tiled=True),
        lax.all_gather(w_dt, "dp", axis=0, tiled=True),
        lax.all_gather(w_bc, "dp", axis=0, tiled=True),
        lax.all_gather(w_out, "dp", axis=0, tiled=True),
    )
    cot_all = lax.all_gather(cotangent, "tensor", axis=0, tiled=True)
    branch_grad = cot_all * live_mask[:, None].astype(jnp.bfloat16)
    out_grad = contract_rows(branch_grad, hidden)
    hidden_grad = jnp.dot(branch_grad, back_out, preferred_element_type=jnp.float32)
    norm_gain_grad = jnp.sum(hidden_grad * gated * scale, axis=0)
    inner_prod = lax.psum(jnp.sum(hidden_grad * gnorm_gain * gated, axis=-1), "tensor")
    gated_grad = scale * gnorm_gain * hidden_grad - gated * scale**3 * (inner_prod / DI)[:, None]
    sigmoid_gate = jax.nn.sigmoid(gate)
    mixed_grad = gated_grad * silu_gate
    gate_grad = gated_grad * mixed * sigmoid_gate * (1.0 + gate * (1.0 - sigmoid_gate))
    inner_grad, state_grad, step_grad, bias_grad, decay_grad, skip_grad = mixer_pullback(mixed_grad)
    state_grad = lax.psum(state_grad, "tensor")
    inner_pre_grad, taps_x_grad, offset_x_grad = inner_pullback(inner_grad)
    state_pre_grad, taps_bc_grad, offset_bc_grad = state_pullback(state_grad)
    gate_low = gate_grad.astype(jnp.bfloat16)
    inner_low = inner_pre_grad.astype(jnp.bfloat16)
    state_low = state_pre_grad.astype(jnp.bfloat16)
    step_low = step_grad.astype(jnp.bfloat16)
    z_grad = contract_rows(tokens, gate_low)
    x_weight_grad = contract_rows(tokens, inner_low)
    dt_weight_grad = contract_rows(tokens, step_low)
    bc_weight_grad = contract_rows(tokens, state_low)
    running = contract_cols(gate_low, back_z)
    running = running + contract_cols(inner_low, back_x)
    normed_grad = lax.psum_scatter(
        running + contract_cols(step_low, back_dt), "tensor", scatter_dimension=0, tiled=True
    )
    own_state = lax.dynamic_slice_in_dim(state_low, start_row, row_count, 0)
    normed_grad = normed_grad + contract_cols(own_state, back_bc)
    gain_part = jnp.sum(normed_grad * resid * inverse, axis=0)
    projected = jnp.sum(normed_grad * in_gain * resid, axis=-1, keepdims=True) / model_width
    x_grad = (
        inverse * in_gain * normed_grad
        - resid * inverse**3 * projected
        + cotangent.astype(jnp.float32)
    )
    w_z_grad, w_x_grad, w_dt_grad, w_bc_grad, w_out_grad = (
        lax.psum_scatter(z_grad, "dp", scatter_dimension=0, tiled=True),
        lax.psum_scatter(x_weight_grad, "dp", scatter_dimension=0, tiled=True),
        lax.psum_scatter(dt_weight_grad, "dp", scatter_dimension=0, tiled=True),
        lax.psum_scatter(bc_weight_grad, "dp", scatter_dimension=0, tiled=True),
        lax.psum_scatter(out_grad, "dp", scatter_dimension=0, tiled=True),
    )
    in_gain_grad = lax.psum_scatter(gain_part, ("dp", "tensor"), scatter_dimension=0, tiled=True)
    small_grads = lax.psum(
        (
            taps_x_grad,
            offset_x_grad,
            taps_bc_grad,
            offset_bc_grad,
            bias_grad,
            decay_grad,
            skip_grad,
            norm_gain_grad,
        ),
        "dp",
    )
    return (
        output,
        x_grad,
        in_gain_grad,
        w_z_grad,
        w_x_grad,
        w_dt_grad,
        w_bc_grad,
        small_grads[0],
        small_grads[1],
        small_grads[2],
        small_grads[3],
        small_grads[4],
        small_grads[5],
        small_grads[6],
        small_grads[7],
        w_out_grad,
    )


def solution(mesh):
    placed = (
        P(("dp", "tensor"), None),
        P(("dp", "tensor"), None),
        P("dp", None),
        P(),
        P("dp", "tensor"),
        P("dp", "tensor"),
        P("dp", "tensor"),
        P("dp", None),
        P(None, "tensor"),
        P("tensor"),
        P(),
        P(),
        P("tensor"),
        P("tensor"),
        P("tensor"),
        P("tensor"),
        P("dp", "tensor"),
    )
    return jax.shard_map(
        local,
        mesh=mesh,
        in_specs=placed,
        out_specs=(
            P(("dp", "tensor"), None),
            P(("dp", "tensor"), None),
            P(("dp", "tensor")),
            P("dp", "tensor"),
            P("dp", "tensor"),
            P("dp", "tensor"),
            P("dp", None),
            P(None, "tensor"),
            P("tensor"),
            P(),
            P(),
            P("tensor"),
            P("tensor"),
            P("tensor"),
            P("tensor"),
            P("dp", "tensor"),
        ),
        check_vma=False,
    )
```

profile of v0, /device:TPU:0, one launch (start us, length us, event | category | flops | bytes accessed | tf_op | source)
XLA Modules:
  0.0 1446.1 jit_solution(2682654118351896735)
XLA Ops:
  16.3 20.2 %all-gather = bf16[16,96,6]{1,2,0:T(8,128)(2,1)S(1)} all-gather(bf16[1,96,6]{1,2,0:T(8,128)(2,1)S(1)} %bitcast.440), channel_id=1, replica_groups=mesh['dp'=16,'tensor'=8] {'dp'}, dimensions={0}, use_global_device_ids=true | all-gather | bytes 19584 | tf_op jit(solution)/shard_map/all_gather | solution.py:136
  36.5 18.4 %all_gather.29 = bf16[1536,256]{1,0:T(8,128)(2,1)S(1)} all-gather(bf16[96,256]{1,0:T(8,128)(2,1)S(1)} %copy-done.22), channel_id=1, replica_groups=mesh['dp'=16,'tensor'=8] {'dp'}, dimensions={0}, use_global_device_ids=true | all-gather | bytes 835584 | tf_op jit(solution)/shard_map/all_gather | solution.py:137
  55.0 48.9 %all-gather.7.cloned.1.call-done = bf16[2048,1536]{1,0:T(8,128)(2,1)} async-done(((bf16[256,1536]{1,0:T(8,128)(2,1)}), bf16[2048,1536]{1,0:T(8,128)(2,1)}) %all-gather.7.cloned.1.call-update) | async-done | bytes 6291472 | tf_op jit(solution)/shard_map/all_gather | solution.py:140
  114.9 21.1 %all-gather.9.cloned.1.call-done = bf16[1536,384]{1,0:T(8,128)(2,1)} async-done(((bf16[96,384]{1,0:T(8,128)(2,1)}), bf16[1536,384]{1,0:T(8,128)(2,1)}) %all-gather.9.cloned.1.call-update) | async-done | bytes 1179664 | tf_op jit(solution)/shard_map/all_gather | solution.py:135
  161.4 181.0 %while.41 = (s32[]{:T(128)}, f32[6,64,128]{2,1,0:T(8,128)S(1)}, f32[8,256,6,64]{1,0,3,2:T(8,128)}, f32[8,6,64,128]{3,2,1,0:T(8,128)}, f32[8]{0:T(128)S(1)}, /*in...) while((s32[]{:T(128)}, f32[6,64,128]{2,1,0:T(8,128)S(1)}, ...), condition=%wide.region_7.8_spmd.clone, body=%wide.region_4.7_spmd.clone.sunk | while | flops 707054592 | bytes 5775740 | solution.py:93
  174.1 9.9 dynamic_update_slice.79
  196.8 9.9 dynamic_update_slice.79
  219.4 9.9 dynamic_update_slice.79
  242.0 10.0 dynamic_update_slice.79
  264.7 9.8 dynamic_update_slice.79
  287.3 9.8 dynamic_update_slice.79
  309.9 9.8 dynamic_update_slice.79
  332.5 9.8 dynamic_update_slice.79
  351.5 10.8 multiply_reduce_fusion.11
  362.3 24.4 %psum.77 = f32[2048]{0:T(1024)S(1)} all-reduce(f32[2048]{0:T(1024)S(1)} %get-tuple-element.816), channel_id=1, replica_groups=mesh['dp'=16,'tensor'=8] {'tensor'}, use_global_device_ids=true, to_apply=%region_9.10 | all-reduce | flops 2048 | bytes 16384 | tf_op jit(solution)/shard_map/psum | solution.py:160
  386.8 10.2 multiply_reduce_fusion.4
  396.9 19.3 %psum.78 = f32[2048]{0:T(1024)S(1)} all-reduce(f32[2048]{0:T(1024)S(1)} %get-tuple-element.731), channel_id=1, replica_groups=mesh['dp'=16,'tensor'=8] {'tensor'}, use_global_device_ids=true, to_apply=%region_12.13 | all-reduce | flops 2048 | bytes 16384 | tf_op jit(solution)/shard_map/psum | solution.py:182
  436.1 315.2 %while.42 = (s32[]{:T(128)}, f32[6,64,128]{2,1,0:T(8,128)S(1)}, f32[8,256,6,64]{1,0,3,2:T(8,128)}, f32[8,256,128]{2,1,0:T(8,128)}, f32[8,256,128]{2,1,0:T(8,128)...) while((s32[]{:T(128)}, f32[6,64,128]{2,1,0:T(8,128)S(1)}, ...), condition=%wide.region_25.26_spmd.clone, body=%wide.region_13.25_spmd.clone.sunk | while | flops 1669436416 | bytes 14925991 | solution.py:93
  505.2 9.8 dynamic_update_slice.84
  544.6 9.8 dynamic_update_slice.84
  662.7 9.8 dynamic_update_slice.84
  797.4 11.5 add_add_fusion
  842.7 18.1 %all-reduce.26.cloned.1.call-done = f32[2048,256]{1,0:T(8,128)} async-done(((f32[2048,256]{1,0:T(8,128)}), f32[2048,256]{1,0:T(8,128)}) %all-reduce.26.cloned.1.call-update) | async-done | bytes 2097168 | tf_op jit(solution)/shard_map/psum | solution.py:188
  871.9 51.2 %reduce-scatter.22.cloned.1.call-done = f32[96,6]{1,0:T(8,128)} async-done(((f32[1536,6]{1,0:T(8,128)}), f32[96,6]{1,0:T(8,128)}) %reduce-scatter.22.cloned.1.call-update) | async-done | bytes 2320
  924.6 54.0 %all-reduce.23 = (f32[4,384]{1,0:T(4,128)}, f32[384]{0:T(512)}, f32[4,256]{1,0:T(4,128)}, f32[256]{0:T(256)}, f32[6]{0:T(128)}, /*index=5*/f32[6]{0:T(128)}, f32[6]{0:T(128)}, f32[384]{0:T(512)}) all-reduce(f32[4,384]{1,0:T(4,128)S(1)} %pad_add_fusion.7, f32[384]{0:T(512)S(1)} %get-tuple-element.740, ...), channel_id=1, replica_groups=mesh['dp'=16,'tensor'=8] {'dp'}, use_global_device_ids=true, to_apply=%region_39.40 | all-reduce | flops 3602 | bytes 28816 | tf_op jit(solution)/shard_map/psum | solution.py:221
  978.6 98.9 %reduce-scatter.12.cloned.1.call-done = f32[256,1536]{1,0:T(8,128)} async-done(((f32[2048,1536]{1,0:T(8,128)}), f32[256,1536]{1,0:T(8,128)}) %reduce-scatter.12.cloned.1.call-update) | async-done | bytes 1572880 | tf_op jit(solution)/shard_map/reduce_scatter | solution.py:201
  1079.7 73.8 %all-reduce.22 = f32[1536]{0:T(1024)S(1)} all-reduce(f32[1536]{0:T(1024)S(1)} %get-tuple-element.741), channel_id=4, replica_groups=mesh['dp'=16,'tensor'=8] {'dp','tensor'}, use_global_device_ids=true, to_apply=%region_30.31.clone | all-reduce | flops 1536 | bytes 12288
  1154.1 25.3 %reduce-scatter.10.cloned.1.call-done = bf16[256,1536]{1,0:T(8,128)(2,1)} async-done(((bf16[2048,1536]{1,0:T(8,128)(2,1)}), bf16[256,1536]{1,0:T(8,128)(2,1)}) %reduce-scatter.10.cloned.1.call-update) | async-done | bytes 786448 | tf_op jit(solution)/shard_map/reduce_scatter | solution.py:163
  1182.9 61.3 %reduce-scatter.20.cloned.1.call-done = f32[96,384]{1,0:T(8,128)} async-done(((f32[1536,384]{1,0:T(8,128)}), f32[96,384]{1,0:T(8,128)}) %reduce-scatter.20.cloned.1.call-update) | async-done | bytes 147472 | tf_op jit(solution)/shard_map/reduce_scatter | solution.py:218
  1244.2 65.7 %reduce-scatter.14.cloned.1.call-done = f32[96,384]{1,0:T(8,128)} async-done(((f32[1536,384]{1,0:T(8,128)}), f32[96,384]{1,0:T(8,128)}) %reduce-scatter.14.cloned.1.call-update) | async-done | bytes 147472 | tf_op jit(solution)/shard_map/reduce_scatter | solution.py:214
  1309.9 65.4 %reduce-scatter.16.cloned.1.call-done = f32[96,384]{1,0:T(8,128)} async-done(((f32[1536,384]{1,0:T(8,128)}), f32[96,384]{1,0:T(8,128)}) %reduce-scatter.16.cloned.1.call-update) | async-done | bytes 147472 | tf_op jit(solution)/shard_map/reduce_scatter | solution.py:215
  1375.3 64.1 %reduce-scatter.18.cloned.1.call-done = f32[96,256]{1,0:T(8,128)} async-done(((f32[1536,256]{1,0:T(8,128)}), f32[96,256]{1,0:T(8,128)}) %reduce-scatter.18.cloned.1.call-update) | async-done | bytes 98320 | tf_op jit(solution)/shard_map/reduce_scatter | solution.py:217
  (753 shorter events, 558.9 us)
Async XLA Ops:
  7.3 96.6 %all-gather.7.cloned.1.call-start = ((), (), s32[]{:S(2)}) async-start(), calls=%async_computation.7 | async-start | bytes 7077888 | tf_op jit(solution)/shard_map/all_gather | solution.py:140
  12.1 123.8 %all-gather.9.cloned.1.call-start = ((), (), s32[]{:S(2)}) async-start(), calls=%async_computation.8 | async-start | bytes 1253376 | tf_op jit(solution)/shard_map/all_gather | solution.py:135
  12.9 338.6 %all-gather.11.cloned.1.call-start = ((), (), s32[]{:S(2)}) async-start(), calls=%async_computation.9 | async-start | bytes 1253376 | tf_op jit(solution)/shard_map/all_gather | solution.py:134
  13.6 373.1 %all-gather.13.cloned.1.call-start = ((), (), s32[]{:S(2)}) async-start(), calls=%async_computation.10 | async-start | bytes 1253376 | tf_op jit(solution)/shard_map/all_gather | solution.py:138
  14.2 372.6 %all-gather.15.cloned.1.call-start = ((), (), s32[]{:S(2)}) async-start(), calls=%async_computation.12 | async-start | bytes 7077888 | tf_op jit(solution)/shard_map/all_gather | solution.py:177
  14.8 846.0 %all-reduce.26.cloned.1.call-start = ((), (), s32[]{:S(2)}) async-start(), calls=%async_computation.14 | async-start | bytes 4194304 | tf_op jit(solution)/shard_map/psum | solution.py:188
  15.3 139.0 %copy-start.42 = (f32[6]{0:T(128)}, f32[6]{0:T(128)S(1)}, u32[]{:S(2)}) copy-start(f32[6]{0:T(128)S(1)} %exponential_negate_fusion) | copy-start | bytes 76
  15.5 92.9 %copy-start.32 = (f32[1,256]{1,0:T(1,128)}, f32[1,256]{1,0:T(1,128)S(1)}, u32[]{:S(2)}) copy-start(f32[1,256]{1,0:T(1,128)S(1)} %get-tuple-element.865) | copy-start | bytes 3076
  15.5 93.0 %copy-start.34 = (f32[1,256]{1,0:T(1,128)}, f32[1,256]{1,0:T(1,128)S(1)}, u32[]{:S(2)}) copy-start(f32[1,256]{1,0:T(1,128)S(1)} %get-tuple-element.866) | copy-start | bytes 3076
  15.5 93.0 %copy-start.36 = (f32[1,256]{1,0:T(1,128)}, f32[1,256]{1,0:T(1,128)S(1)}, u32[]{:S(2)}) copy-start(f32[1,256]{1,0:T(1,128)S(1)} %get-tuple-element.867) | copy-start | bytes 3076
  15.5 92.9 %copy-start.38 = (f32[1,256]{1,0:T(1,128)}, f32[1,256]{1,0:T(1,128)S(1)}, u32[]{:S(2)}) copy-start(f32[1,256]{1,0:T(1,128)S(1)} %get-tuple-element.868) | copy-start | bytes 3076
  15.7 371.1 %copy-start.44 = (bf16[2048]{0:T(1024)(128)(2,1)}, bf16[2048]{0:T(1024)(128)(2,1)S(1)}, u32[]{:S(2)}) copy-start(bf16[2048]{0:T(1024)(128)(2,1)S(1)} %convert_element_type.111) | copy-start | bytes 12292
  16.2 125.5 %copy-start.24 = (f32[384]{0:T(512)}, f32[384]{0:T(512)S(1)}, u32[]{:S(2)}) copy-start(f32[384]{0:T(512)S(1)} %get-tuple-element.745) | copy-start | bytes 4612
  16.2 125.5 %copy-start.26 = (f32[384]{0:T(512)}, f32[384]{0:T(512)S(1)}, u32[]{:S(2)}) copy-start(f32[384]{0:T(512)S(1)} %get-tuple-element.746) | copy-start | bytes 4612
  16.3 125.5 %copy-start.28 = (f32[384]{0:T(512)}, f32[384]{0:T(512)S(1)}, u32[]{:S(2)}) copy-start(f32[384]{0:T(512)S(1)} %get-tuple-element.747) | copy-start | bytes 4612
  55.0 53.5 %copy-start.11 = (bf16[1536,256]{1,0:T(8,128)(2,1)}, bf16[1536,256]{1,0:T(8,128)(2,1)S(1)}, u32[]{:S(2)}) copy-start(bf16[1536,256]{1,0:T(8,128)(2,1)S(1)} %all_gather.29) | copy-start | bytes 2359300
  55.0 54.8 %copy-start.54 = (f32[256]{0:T(256)S(1)}, f32[256]{0:T(256)}, u32[]{:S(2)}) copy-start(f32[256]{0:T(256)} %param.32) | copy-start | bytes 3076
  146.1 205.3 %copy-start.2 = (bf16[2048,384]{1,0:T(8,128)(2,1)}, bf16[2048,384]{1,0:T(8,128)(2,1)S(1)}, u32[]{:S(2)}) copy-start(bf16[2048,384]{1,0:T(8,128)(2,1)S(1)} %get-tuple-element.820) | copy-start | bytes 4718596
  351.5 35.3 %copy-start.49 = (f32[384]{0:T(512)S(1)}, f32[384]{0:T(512)}, u32[]{:S(2)}) copy-start(f32[384]{0:T(512)} %param.36) | copy-start | bytes 4612
  755.1 167.9 %reduce-scatter.22.cloned.1.call-start = ((), (), s32[]{:S(2)}) async-start(), calls=%async_computation.19 | async-start | bytes 835584
  782.4 295.1 %reduce-scatter.12.cloned.1.call-start = ((), (), s32[]{:S(2)}) async-start(), calls=%async_computation.13 | async-start | bytes 14155776 | tf_op jit(solution)/shard_map/reduce_scatter | solution.py:201
  808.9 370.4 %reduce-scatter.10.cloned.1.call-start = ((), (), s32[]{:S(2)}) async-start(), calls=%async_computation.11 | async-start | bytes 7077888 | tf_op jit(solution)/shard_map/reduce_scatter | solution.py:163
  817.5 426.6 %reduce-scatter.20.cloned.1.call-start = ((), (), s32[]{:S(2)}) async-start(), calls=%async_computation.18 | async-start | bytes 2506752 | tf_op jit(solution)/shard_map/reduce_scatter | solution.py:218
  826.9 483.0 %reduce-scatter.14.cloned.1.call-start = ((), (), s32[]{:S(2)}) async-start(), calls=%async_computation.15 | async-start | bytes 2506752 | tf_op jit(solution)/shard_map/reduce_scatter | solution.py:214
  834.8 540.5 %reduce-scatter.16.cloned.1.call-start = ((), (), s32[]{:S(2)}) async-start(), calls=%async_computation.16 | async-start | bytes 2506752 | tf_op jit(solution)/shard_map/reduce_scatter | solution.py:215
  842.5 596.8 %reduce-scatter.18.cloned.1.call-start = ((), (), s32[]{:S(2)}) async-start(), calls=%async_computation.17 | async-start | bytes 1671168 | tf_op jit(solution)/shard_map/reduce_scatter | solution.py:217
  867.7 56.9 %copy-start.53 = (f32[384]{0:T(512)S(1)}, f32[384]{0:T(512)}, u32[]{:S(2)}) copy-start(f32[384]{0:T(512)} %get-tuple-element.730) | copy-start | bytes 4612
  867.7 209.8 %copy-start.5 = (bf16[256,1536]{1,0:T(8,128)(2,1)S(1)}, bf16[256,1536]{1,0:T(8,128)(2,1)}, u32[]{:S(2)}) copy-start(bf16[256,1536]{1,0:T(8,128)(2,1)} %param.21) | copy-start | bytes 2359300
  867.7 209.8 %copy-start.12 = (bf16[1536,256]{1,0:T(8,128)(2,1)S(1)}, bf16[1536,256]{1,0:T(8,128)(2,1)}, u32[]{:S(2)}) copy-start(bf16[1536,256]{1,0:T(8,128)(2,1)} %copy-done.11) | copy-start | bytes 2359300
  867.7 209.8 %copy-start.21 = (f32[1536]{0:T(1024)S(1)}, f32[1536]{0:T(1024)}, u32[]{:S(2)}) copy-start(f32[1536]{0:T(1024)} %param.24) | copy-start | bytes 18436
  867.7 209.8 %copy-start.31 = (f32[256]{0:T(256)S(1)}, f32[256]{0:T(256)}, u32[]{:S(2)}) copy-start(f32[256]{0:T(256)} %copy-done.30) | copy-start | bytes 3076
  870.8 308.5 %copy-start.47 = (f32[256]{0:T(256)S(1)}, f32[256]{0:T(256)}, u32[]{:S(2)}) copy-start(f32[256]{0:T(256)} %get-tuple-element.869) | copy-start | bytes 3076
  (45 other events, 264.5 us)
Sparse Core Ops, SparseCore 0:
  12.2 91.5 all-gather.6
  105.5 30.3 all-gather.8
  137.6 32.7 all-gather.10
  172.0 32.6 all-gather.12
  206.9 89.2 all-gather.14
  755.2 105.5 all-reduce.25
  863.7 59.2 reduce-scatter.21
  927.4 150.0 reduce-scatter.11
  1081.8 97.4 reduce-scatter.9
  1182.3 61.8 reduce-scatter.19
  1247.3 62.5 reduce-scatter.13
  1312.9 62.3 reduce-scatter.15
  1378.4 60.9 reduce-scatter.17
where the time goes:
time: 1460 us; the launch traced here: 1450 us
  waiting for transfers between devices  523 us (36%)
  local copies, waits for them, and re-layouts  272 us (19%)
  matrix products  261 us (18%)
  blocking collectives  210 us (14%)
  other arithmetic  163 us (11%)
  between operations  14.9 us (1%)
    dynamic_update_slice x40, local copies, waits for them, and re-layouts, state_space(): lax.scan(jax.checkpoint(advance), start, (x_blocks, b_blocks, c_blocks, s...  164 us
    reduce_scatter x1, waiting for transfers between devices, local(): lax.psum_scatter(running + contract_cols(step_low, back_dt), 'tensor', sc...  98.9 us
    another operation x59, other arithmetic  97 us
    unnamed x1, blocking collectives  73.8 us
    reduce_scatter x1, waiting for transfers between devices, local(): lax.psum_scatter(z_grad, 'dp', scatter_dimension=0, tiled=True)  65.7 us
    reduce_scatter x1, waiting for transfers between devices, local(): lax.psum_scatter(x_weight_grad, 'dp', scatter_dimension=0, tiled=True)  65.4 us
    reduce_scatter x1, waiting for transfers between devices, local(): lax.psum_scatter(bc_weight_grad, 'dp', scatter_dimension=0, tiled=True)  64.1 us
    reduce_scatter x1, waiting for transfers between devices, local(): lax.psum_scatter(out_grad, 'dp', scatter_dimension=0, tiled=True)  61.3 us
  transfers between devices with their start and end apart: 13, of which 10 were waited for; matrix products, arithmetic and copies ran while one was open for 23% of the time, Pallas kernels for 0%

commit v1 on v0

v1 whole, which is shorter than its diff:
```python
import functools

import jax
import jax.numpy as jnp
from jax import lax
from jax.experimental import pallas as pl
from jax.experimental.pallas import tpu as pltpu
from jax.sharding import PartitionSpec as P

Q = 256
HD = 64
NS = 128
EPS = 1e-05
F32 = jnp.float32
BF = jnp.bfloat16
VMEM_LIMIT = 56 * 1024 * 1024


def mm(a, b):
    return lax.dot_general(a, b, (((1,), (0,)), ((), ())), preferred_element_type=F32)


def mm_nt(a, b):
    return lax.dot_general(a, b, (((1,), (1,)), ((), ())), preferred_element_type=F32)


def mm_tn(a, b):
    return lax.dot_general(a, b, (((0,), (0,)), ((), ())), preferred_element_type=F32)


def split3(v):
    hi = v.astype(BF)
    rest = v - hi.astype(F32)
    mid = rest.astype(BF)
    low = (rest - mid.astype(F32)).astype(BF)
    return hi, mid, low


def split2(v):
    hi = v.astype(BF)
    return hi, (v - hi.astype(F32)).astype(BF)


def lanes(shape):
    return lax.broadcasted_iota(jnp.int32, shape, len(shape) - 1)


def lower_ones():
    rows = lax.broadcasted_iota(jnp.int32, (Q, Q), 0)
    return rows >= lanes((Q, Q))


def expander(heads):
    row = lax.broadcasted_iota(jnp.int32, (128, heads * HD), 0)
    head = lanes((128, heads * HD)) // HD
    return ((row == head) | (row == head + 8)).astype(BF)


def spread(v, ones):
    hi, low = split2(v)
    first = lanes(v.shape) < 8
    return mm(jnp.where(first, hi.astype(F32), low.astype(F32)).astype(BF), ones)


def gather_heads(v, ones):
    hi, low = split2(v)
    return mm_nt(hi, ones) + mm_nt(low, ones)


def softplus(z):
    return jnp.maximum(z, 0.0) + jnp.log1p(jnp.exp(-jnp.abs(z)))


def sigmoid(v):
    return 1.0 / (1.0 + jnp.exp(-v))


def running_sum(tri, v):
    hi, mid, low = split3(v)
    return mm(tri, hi) + mm(tri, mid) + mm(tri, low)


def suffix_sum(tri, v):
    hi, mid, low = split3(v)
    return mm_tn(tri, hi) + mm_tn(tri, mid) + mm_tn(tri, low)


def forward_kernel(
    keep_ref, tok_ref, w_ref, conv_ref, head_ref, chan_ref, ones_ref, tri_ref,
    gate_ref, pre_ref, act_ref, z_ref, cum_ref, mixed_ref, sin_ref,
    state, tail, buf, *, heads,
):
    c = pl.program_id(0)
    width = heads * HD
    conv = width + 2 * NS

    @pl.when(c == 0)
    def _():
        state[...] = jnp.zeros_like(state)
        tail[...] = jnp.zeros_like(tail)

    keep = keep_ref[c].astype(F32)
    proj = mm(tok_ref[...], w_ref[...])
    gate_ref[...] = proj[:, :width]
    pre = proj[:, width : width + conv]
    pre_ref[...] = pre
    buf[0:8, :] = tail[...] * keep
    buf[8 : 8 + Q, :] = pre
    tail[...] = pre[Q - 8 :, :]
    run = conv_ref[4:5, :] + conv_ref[3:4, :] * pre
    for j in range(1, 4):
        run = run + conv_ref[3 - j : 4 - j, :] * buf[8 - j : 8 - j + Q, :]
    act = (run * sigmoid(run)).astype(BF)
    act_ref[...] = act
    z = proj[:, width + conv :] + head_ref[0:1, :]
    z_ref[...] = z
    step = softplus(z)
    tri = tri_ref[...]
    cum = running_sum(tri, step * head_ref[1:2, :])
    cum_ref[...] = cum
    ones = ones_ref[...]
    step_x = spread(step, ones)
    grow_x = spread(jnp.exp(cum), ones)
    fade_x = spread(jnp.exp(cum[Q - 1 :, :] - cum), ones)
    x = act[:, :width].astype(F32)
    xs = x * step_x
    bmat = act[:, width : width + NS]
    cmat = act[:, width + NS :]
    scores = mm_nt(cmat, bmat)
    cum_row = cum.T
    lower = lower_ones()
    half = lanes((Q, 128)) < HD
    carried = state[...] * keep
    sin_ref[...] = carried
    through = mm(cmat, carried.astype(BF)) * grow_x
    for p in range(heads // 2):
        span = slice(128 * p, 128 * (p + 1))
        xp = xs[:, span]
        total = through[:, span] + chan_ref[0:1, span] * x[:, span]
        for k in range(2):
            h = 2 * p + k
            diff = cum[:, h : h + 1] - cum_row[h : h + 1, :]
            decay = jnp.exp(jnp.where(lower, diff, -1e30))
            mix = (scores * decay).astype(BF)
            mine = half if k == 0 else ~half
            total = total + mm(mix, jnp.where(mine, xp, 0.0).astype(BF))
        mixed_ref[:, span] = total
    state[...] = carried * grow_x[Q - 1 :, :] + mm_tn(bmat, (xs * fade_x).astype(BF))


def forward(keep, tokens, weights, conv, head, chan, ones, tri, heads):
    rows, d = tokens.shape
    n = rows // Q
    width = heads * HD
    cols = width + 2 * NS
    block = lambda w: pl.BlockSpec((Q, w), lambda c, keep: (c, 0))
    whole = lambda a: pl.BlockSpec(a.shape, lambda c, keep: (0,) * a.ndim)
    out = lambda w, dt: jax.ShapeDtypeStruct((rows, w), dt)
    return pl.pallas_call(
        functools.partial(forward_kernel, heads=heads),
        grid_spec=pltpu.PrefetchScalarGridSpec(
            num_scalar_prefetch=1,
            grid=(n,),
            in_specs=[
                block(d),
                pl.BlockSpec((d, width + cols + 128), lambda c, keep: (0, 0)),
                whole(conv), whole(head), whole(chan), whole(ones), whole(tri),
            ],
            out_specs=[
                block(width), block(cols), block(cols), block(128), block(128), block(width),
                pl.BlockSpec((NS, width), lambda c, keep: (c, 0)),
            ],
            scratch_shapes=[
                pltpu.VMEM((NS, width), F32),
                pltpu.VMEM((8, cols), F32),
                pltpu.VMEM((8 + Q, cols), F32),
            ],
        ),
        out_shape=[
            out(width, F32), out(cols, F32), out(cols, BF), out(128, F32), out(128, F32), out(width, F32),
            jax.ShapeDtypeStruct((n * NS, width), F32),
        ],
        compiler_params=pltpu.CompilerParams(
            dimension_semantics=("arbitrary",), vmem_limit_bytes=VMEM_LIMIT
        ),
        cost_estimate=pl.CostEstimate(flops=12 * 10**9, bytes_accessed=30 * 10**6, transcendentals=5 * 10**6),
        name="ssd_forward",
    )(keep, tokens, weights, conv, head, chan, ones, tri)


def grad_sums_kernel(live_ref, cot_ref, w_ref, mixed_ref, gate_ref, chan_ref, hg_ref, sums_ref):
    c = pl.program_id(0)
    width = mixed_ref.shape[1]
    row = lax.broadcasted_iota(jnp.int32, (Q, width), 0)
    hg = jnp.where(row < live_ref[c], mm(cot_ref[...], w_ref[...]), 0.0)
    hg_ref[...] = hg
    gate = gate_ref[...]
    gated = mixed_ref[...] * (gate * sigmoid(gate))
    one = jnp.ones((8, width), BF)
    square = sum(mm_nt(one, part) for part in split2(gated * gated))
    inner = sum(mm_nt(one, part) for part in split2(hg * chan_ref[1:2, :] * gated))
    first = lax.broadcasted_iota(jnp.int32, (8, Q), 0) == 0
    sums_ref[...] = jnp.where(first, square, inner)


def grad_sums(live, cot, weights, mixed, gate, chan, first_col):
    rows, d = cot.shape
    width = mixed.shape[1]
    block = lambda w: pl.BlockSpec((Q, w), lambda c, live: (c, 0))
    return pl.pallas_call(
        grad_sums_kernel,
        grid_spec=pltpu.PrefetchScalarGridSpec(
            num_scalar_prefetch=1,
            grid=(rows // Q,),
            in_specs=[
                block(d),
                pl.BlockSpec((d, width), lambda c, live: (0, first_col // width)),
                block(width), block(width),
                pl.BlockSpec(chan.shape, lambda c, live: (0, 0)),
            ],
            out_specs=[block(width), pl.BlockSpec((8, Q), lambda c, live: (0, c))],
        ),
        out_shape=[jax.ShapeDtypeStruct((rows, width), F32), jax.ShapeDtypeStruct((8, rows), F32)],
        compiler_params=pltpu.CompilerParams(
            dimension_semantics=("arbitrary",), vmem_limit_bytes=VMEM_LIMIT
        ),
        cost_estimate=pl.CostEstimate(flops=2 * rows * d * width, bytes_accessed=17 * 10**6, transcendentals=10**6),
        name="grad_sums",
    )(live, cot, weights, mixed, gate, chan)


def gate_back_kernel(live_ref, hg_ref, mixed_ref, gate_ref, sums_ref, chan_ref, hidden_ref, glow_ref, dy_ref, ngg_ref, *, inner):
    c = pl.program_id(0)
    width = mixed_ref.shape[1]

    @pl.when(c == 0)
    def _():
        ngg_ref[...] = jnp.zeros_like(ngg_ref)

    sums = sums_ref[...]
    scale_row = lax.rsqrt(sums[0:1, :] / inner + EPS)
    pull_row = scale_row * scale_row * scale_row * (sums[1:2, :] / inner)
    sub = lax.broadcasted_iota(jnp.int32, (128, Q), 0)
    cols = jnp.where(sub == 0, scale_row, jnp.where(sub == 1, pull_row, 0.0)).T
    scale = cols[:, 0:1]
    pull = cols[:, 1:2]
    hg = hg_ref[...]
    mixed = mixed_ref[...]
    gate = gate_ref[...]
    sg = sigmoid(gate)
    silu = gate * sg
    gated = mixed * silu
    normal = gated * scale
    gain = chan_ref[1:2, :]
    row = lax.broadcasted_iota(jnp.int32, (Q, width), 0)
    hidden_ref[...] = jnp.where(row < live_ref[c], normal * gain, 0.0).astype(BF)
    ngg_ref[0:1, :] += jnp.sum(hg * normal, axis=0, keepdims=True)
    gg = scale * gain * hg - gated * pull
    dy_ref[...] = gg * silu
    glow_ref[...] = (gg * mixed * sg * (1.0 + gate * (1.0 - sg))).astype(BF)


def gate_back(live, hg, mixed, gate, sums, chan, inner):
    rows, width = hg.shape
    block = lambda w: pl.BlockSpec((Q, w), lambda c, live: (c, 0))
    return pl.pallas_call(
        functools.partial(gate_back_kernel, inner=inner),
        grid_spec=pltpu.PrefetchScalarGridSpec(
            num_scalar_prefetch=1,
            grid=(rows // Q,),
            in_specs=[
                block(width), block(width), block(width),
                pl.BlockSpec((8, Q), lambda c, live: (0, c)),
                pl.BlockSpec(chan.shape, lambda c, live: (0, 0)),
            ],
            out_specs=[block(width), block(width), block(width), pl.BlockSpec((8, width), lambda c, live: (0, 0))],
        ),
        out_shape=[
            jax.ShapeDtypeStruct((rows, width), BF), jax.ShapeDtypeStruct((rows, width), BF),
            jax.ShapeDtypeStruct((rows, width), F32), jax.ShapeDtypeStruct((8, width), F32),
        ],
        compiler_params=pltpu.CompilerParams(
            dimension_semantics=("arbitrary",), vmem_limit_bytes=VMEM_LIMIT
        ),
        cost_estimate=pl.CostEstimate(flops=20 * rows * width, bytes_accessed=16 * 10**6, transcendentals=10**6),
        name="gate_back",
    )(live, hg, mixed, gate, sums, chan)


def backward_kernel(
    keep_ref, act_ref, pre_ref, before_ref, z_ref, cum_ref, sin_ref, dy_ref, conv_ref, head_ref, chan_ref, ones_ref, tri_ref,
    low_ref, convsum_ref, headsum_ref, skipsum_ref,
    dstate, halo, buf, *, heads, count,
):
    c = count - 1 - pl.program_id(0)
    width = heads * HD

    @pl.when(pl.program_id(0) == 0)
    def _():
        dstate[...] = jnp.zeros_like(dstate)
        halo[...] = jnp.zeros_like(halo)
        convsum_ref[...] = jnp.zeros_like(convsum_ref)
        headsum_ref[...] = jnp.zeros_like(headsum_ref)
        skipsum_ref[...] = jnp.zeros_like(skipsum_ref)

    keep = keep_ref[c].astype(F32)
    keep_next = keep_ref[c + 1].astype(F32)
    act = act_ref[...]
    x = act[:, :width].astype(F32)
    bmat = act[:, width : width + NS]
    cmat = act[:, width + NS :]
    z = z_ref[...]
    step = softplus(z)
    cum = cum_ref[...]
    ones = ones_ref[...]
    tri = tri_ref[...]
    step_x = spread(step, ones)
    grow_x = spread(jnp.exp(cum), ones)
    fade_x = spread(jnp.exp(cum[Q - 1 :, :] - cum), ones)
    xs = x * step_x
    xsb = xs.astype(BF)
    dy = dy_ref[...]
    scores = mm_nt(cmat, bmat)
    cum_row = cum.T
    lower = lower_ones()
    lane = lanes((Q, 128))
    half = lane < HD
    sub = lax.broadcasted_iota(jnp.int32, (128, Q), 0)
    dscores = jnp.zeros((Q, Q), F32)
    rowsum = jnp.zeros((Q, 128), F32)
    colsum = jnp.zeros((128, Q), F32)
    parts = []
    for p in range(heads // 2):
        span = slice(128 * p, 128 * (p + 1))
        dyp = dy[:, span]
        part = jnp.zeros((Q, 128), F32)
        for k in range(2):
            h = 2 * p + k
            diff = cum[:, h : h + 1] - cum_row[h : h + 1, :]
            decay = jnp.exp(jnp.where(lower, diff, -1e30))
            mix = (scores * decay).astype(BF)
            mine = half if k == 0 else ~half
            dym = jnp.where(mine, dyp, 0.0).astype(BF)
            grad = mm_nt(dym, xsb[:, span]) * decay
            dscores = dscores + grad
            grad = grad * scores
            rowsum = jnp.where(lane == h, jnp.sum(grad, axis=1, keepdims=True), rowsum)
            colsum = jnp.where(sub == h, jnp.sum(grad, axis=0, keepdims=True), colsum)
            part = part + mm_tn(mix, dym)
        parts.append(part)
    within = jnp.concatenate(parts, axis=1)
    carried = sin_ref[...]
    carried_low = carried.astype(BF)
    dstate_now = dstate[...]
    dstate_low = dstate_now.astype(BF)
    dyg = (dy * grow_x).astype(BF)
    dsl = dscores.astype(BF)
    dc = mm(dsl, bmat) + mm_nt(dyg, carried_low)
    xsf = (xs * fade_x).astype(BF)
    db = mm_tn(dsl, cmat) + mm_nt(xsf, dstate_low)
    through = mm(cmat, carried_low) * grow_x
    later = mm(bmat, dstate_low) * fade_x
    last_x = grow_x[Q - 1 :, :]
    q_through = gather_heads(dy * through, ones)
    q_later = gather_heads(x * later, ones)
    q_within = gather_heads(x * within, ones)
    hold = jnp.sum(dstate_now * carried, axis=0, keepdims=True) * last_x
    q_hold = gather_heads(jnp.broadcast_to(hold, (8, width)), ones)[0:1, :]
    dstate[...] = (mm_tn(cmat, dyg) + last_x * dstate_now) * keep
    dxs = within + later
    dx = step_x * dxs + chan_ref[0:1, :] * dy
    first = lane < 8
    net = jnp.where(first, q_through + rowsum - colsum.T, 0.0)
    push = step * q_later
    drate = suffix_sum(tri, net) + running_sum(tri, push) - push + q_hold
    rate_of = head_ref[1:2, :]
    dstep = q_within + q_later + drate * rate_of
    dz = jnp.where(lane < heads, dstep * sigmoid(z), 0.0)
    headsum_ref[0:1, :] += jnp.sum(dz, axis=0, keepdims=True)
    headsum_ref[1:2, :] += jnp.sum(drate * step * rate_of, axis=0, keepdims=True)
    skipsum_ref[0:1, :] += jnp.sum(dy * x, axis=0, keepdims=True)

    grad = jnp.concatenate([dx, db, dc], axis=1)
    buf[0:8, :] = before_ref[...] * keep
    buf[8 : 8 + Q, :] = pre_ref[...]
    run = conv_ref[4:5, :] + conv_ref[3:4, :] * buf[8 : 8 + Q, :]
    for j in range(1, 4):
        run = run + conv_ref[3 - j : 4 - j, :] * buf[8 - j : 8 - j + Q, :]
    sg = sigmoid(run)
    dact = grad * (sg * (1.0 + run * (1.0 - sg)))
    for j in range(4):
        convsum_ref[3 - j : 4 - j, :] += jnp.sum(dact * buf[8 - j : 8 - j + Q, :], axis=0, keepdims=True)
    convsum_ref[4:5, :] += jnp.sum(dact, axis=0, keepdims=True)
    buf[0:Q, :] = dact
    buf[Q : Q + 8, :] = halo[...] * keep_next
    halo[...] = dact[0:8, :]
    dpre = conv_ref[3:4, :] * dact
    for j in range(1, 4):
        dpre = dpre + conv_ref[3 - j : 4 - j, :] * buf[j : j + Q, :]
    low_ref[:, : width + 2 * NS] = dpre.astype(BF)
    low_ref[:, width + 2 * NS :] = dz.astype(BF)


def backward(keep, act, pre, z, cum, sin, dy, conv, head, chan, ones, tri, heads):
    rows, cols = act.shape
    n = rows // Q
    width = heads * HD
    at = lambda i: n - 1 - i
    block = lambda w: pl.BlockSpec((Q, w), lambda i, keep: (at(i), 0))
    whole = lambda a: pl.BlockSpec(a.shape, lambda i, keep: (0,) * a.ndim)
    still = lambda w: pl.BlockSpec((8, w), lambda i, keep: (0, 0))
    return pl.pallas_call(
        functools.partial(backward_kernel, heads=heads, count=n),
        grid_spec=pltpu.PrefetchScalarGridSpec(
            num_scalar_prefetch=1,
            grid=(n,),
            in_specs=[
                block(cols), block(cols),
                pl.BlockSpec((8, cols), lambda i, keep: (jnp.maximum(at(i) * (Q // 8) - 1, 0), 0)),
                block(128), block(128),
                pl.BlockSpec((NS, width), lambda i, keep: (at(i), 0)),
                block(width),
                whole(conv), whole(head), whole(chan), whole(ones), whole(tri),
            ],
            out_specs=[block(cols + 128), still(cols), still(128), still(width)],
            scratch_shapes=[
                pltpu.VMEM((NS, width), F32),
                pltpu.VMEM((8, cols), F32),
                pltpu.VMEM((8 + Q, cols), F32),
            ],
        ),
        out_shape=[
            jax.ShapeDtypeStruct((rows, cols + 128), BF),
            jax.ShapeDtypeStruct((8, cols), F32), jax.ShapeDtypeStruct((8, 128), F32), jax.ShapeDtypeStruct((8, width), F32),
        ],
        compiler_params=pltpu.CompilerParams(
            dimension_semantics=("arbitrary",), vmem_limit_bytes=VMEM_LIMIT
        ),
        cost_estimate=pl.CostEstimate(flops=30 * 10**9, bytes_accessed=25 * 10**6, transcendentals=6 * 10**6),
        name="ssd_backward",
    )(keep, act, pre, pre, z, cum, sin, dy, conv, head, chan, ones, tri)


def ring_maps(size, step):
    places = size // 2
    return [(t, ((t // 2 + step) % places) * 2 + t % 2) for t in range(size)]


ZR, ZL = ring_maps(8, 1), ring_maps(8, -1)
YS = [(t, t ^ 1) for t in range(8)]
ZN, ZF = [(t, t ^ 2) for t in range(8)], [(t, t ^ 4) for t in range(8)]
XR = [(d, d // 8 * 8 + (d % 8 // 2 + 1) % 4 * 2 + d % 2) for d in range(16)]
XL = [(d, d // 8 * 8 + (d % 8 // 2 + 3) % 4 * 2 + d % 2) for d in range(16)]
CS = [(d, d ^ 1) for d in range(16)]
XN, XF = [(d, d ^ 2) for d in range(16)], [(d, d ^ 4) for d in range(16)]
YL = [(d, d ^ 8) for d in range(16)]
FRONT = 160


def pick(array, index, axis):
    return lax.dynamic_index_in_dim(array, index, axis, keepdims=False)


def gather_tensor(x):
    t = lax.axis_index("tensor")
    z, y = t // 2, t % 2
    send = lambda v, to: lax.ppermute(v, "tensor", to)
    a, b = x[:FRONT], x[FRONT:]
    nb = b.shape[0] // 2
    out = jnp.zeros((8 * Q, x.shape[1]), x.dtype)

    def put(out, piece, dz, dy, row):
        at = (((z + dz) % 4) * 2 + (y + dy) % 2) * Q + row
        return lax.dynamic_update_slice_in_dim(out, piece, at, 0)

    b_right, b_left = send(b, ZR), send(b, ZL)
    a_y = send(a, YS)
    out = put(out, x, 0, 0, 0)
    b_far = jnp.concatenate([send(b_right[:nb], ZR), send(b_left[nb:], ZL)])
    a_right, a_left = send(a, ZR), send(a, ZL)
    ay_right, ay_left = send(a_y, ZR), send(a_y, ZL)
    far = send(a_right, ZR), send(ay_left, ZL)
    by = send(jnp.concatenate([b, b_right, b_left]), YS)
    by_far = send(b_far, YS)
    size = b.shape[0]
    out = put(out, a_y, 0, 1, 0)
    out = put(out, by[:size], 0, 1, FRONT)
    out = put(out, jnp.concatenate([a_right, b_right]), -1, 0, 0)
    out = put(out, jnp.concatenate([a_left, b_left]), 1, 0, 0)
    out = put(out, jnp.concatenate([ay_right, by[size : 2 * size]]), -1, 1, 0)
    out = put(out, jnp.concatenate([ay_left, by[2 * size :]]), 1, 1, 0)
    out = put(out, jnp.concatenate([far[0], b_far]), 2, 0, 0)
    out = put(out, jnp.concatenate([far[1], by_far]), 2, 1, 0)
    return out


def ring_sum(block, right, left, send):
    up = lambda v: v.astype(F32)
    far = block(2)
    from_left, from_right = send(far[0], right), send(far[1], left)
    ahead, behind = block(1), block(3)
    ahead = jnp.stack([(up(ahead[0]) + up(from_left)).astype(BF), ahead[1]])
    behind = jnp.stack([behind[0], (up(behind[1]) + up(from_right)).astype(BF)])
    return up(block(0)) + up(send(ahead, right)) + up(send(behind, left))


def scatter_tensor(part):
    t = lax.axis_index("tensor")
    z, y = t // 2, t % 2
    d = part.shape[1]
    send = lambda v, to: lax.ppermute(v, "tensor", to)
    stack = part.reshape(4, 2, Q, d)
    front, back = stack[:, :, :FRONT], stack[:, :, FRONT:]
    other = pick(back, 1 - y, 1)
    back = (pick(back, y, 1).astype(F32) + send(other, YS).astype(F32)).astype(BF)
    back = back.reshape(4, 2, (Q - FRONT) // 2, d)
    front = ring_sum(lambda k: pick(front, (z + k) % 4, 0), ZR, ZL, send)
    back = ring_sum(lambda k: pick(back, (z + k) % 4, 0), ZR, ZL, send)
    front = pick(front, y, 0) + send(pick(front, 1 - y, 0).astype(BF), YS).astype(F32)
    return jnp.concatenate([front, back.reshape(Q - FRONT, d)])


def scatter_dp(part):
    i = lax.axis_index("dp")
    yl, x, core = i // 8, i % 8 // 2, i % 2
    send = lambda v, to: lax.ppermute(v, "dp", to)
    rows, cols = part.shape
    stack = part.reshape(2, 4, 2, rows // 16, cols)
    both = (pick(stack, core, 2).astype(F32) + send(pick(stack, 1 - core, 2), CS).astype(F32)).astype(BF)
    own = ring_sum(lambda k: pick(both, (x + k) % 4, 1), XR, XL, send)
    return pick(own, yl, 0) + send(pick(own, 1 - yl, 0).astype(BF), YL).astype(F32)


def total(value, axis, maps):
    for to in maps:
        value = value + lax.ppermute(value, axis, to)
    return value


def local(
    x_in,
    cotangent,
    seq_lengths,
    in_gain,
    w_z,
    w_x,
    w_dt,
    w_bc,
    conv_wx,
    conv_bx,
    conv_wbc,
    conv_bbc,
    dt_bias,
    a_log,
    d_skip,
    gnorm_gain,
    w_out,
):
    rows, d = x_in.shape
    heads = dt_bias.shape[0]
    width = heads * HD
    cols = width + 2 * NS
    inner = width * 8
    own = w_z.shape[0]
    t = lax.axis_index("tensor")
    dp = lax.axis_index("dp")

    lengths = seq_lengths[0]
    spans = (lengths + Q - 1) // Q * Q
    starts = jnp.cumsum(spans) - spans
    place = jnp.arange(9, dtype=jnp.int32)[:, None] * Q
    inside = (place >= starts) & (place < starts + spans)
    keep = jnp.sum((inside & (place > starts)).astype(jnp.int32), axis=1)
    live = jnp.sum(jnp.where(inside, jnp.clip(starts + lengths - place, 0, Q), 0), axis=1)

    resid = x_in.astype(F32)
    inverse = lax.rsqrt(jnp.mean(resid * resid, axis=-1, keepdims=True) + EPS)
    normed = (resid * inverse * in_gain).astype(BF)
    tokens = gather_tensor(normed)

    blank = lambda k: jnp.zeros((own, k), BF)
    dt_cols = jnp.concatenate([w_dt, blank(8 - heads), w_dt, blank(120 - heads)], axis=1)
    own_in = jnp.concatenate([w_z, w_x, w_bc, dt_cols], axis=1)
    weights = lax.all_gather(jnp.concatenate([own_in, w_out], axis=1), "dp", axis=0, tiled=True)
    split = own_in.shape[1]

    def pad_rows(*values):
        stack = jnp.concatenate([v.reshape(-1, v.shape[-1]) for v in values])
        return jnp.pad(stack, ((0, 8 - stack.shape[0]), (0, 0)))

    def per_head(v):
        gap = jnp.zeros((8 - heads,), F32)
        return jnp.concatenate([v, gap, v, gap, jnp.zeros((112,), F32)])

    conv = pad_rows(jnp.concatenate([conv_wx, conv_wbc], axis=1), jnp.concatenate([conv_bx, conv_bbc]))
    head = pad_rows(per_head(dt_bias), per_head(-jnp.exp(a_log)))
    chan = pad_rows(jnp.repeat(d_skip, HD), gnorm_gain)
    ones = expander(heads)
    tri = lower_ones().astype(BF)

    gate, pre, act, z, cum, mixed, sin = forward(keep, tokens, weights, conv, head, chan, ones, tri, heads)
    late, _ = lax.optimization_barrier((cotangent, tokens[:8]))
    cot_all = gather_tensor(late)
    hg, sums = grad_sums(live, cot_all, weights, mixed, gate, chan, split)
    sums = total(sums, "tensor", (YS, ZN, ZF))
    hidden, gate_low, dy, gain_sum = gate_back(live, hg, mixed, gate, sums, chan, inner)
    full_in, full_out = weights[:, :split], weights[:, split:]
    branch = scatter_tensor(mm_nt(hidden, full_out).astype(BF))
    own_live = pick(live, t, 0)
    live_rows = jnp.arange(rows, dtype=jnp.int32)[:, None] < own_live
    output = (resid + jnp.where(live_rows, branch, 0.0)).astype(BF)

    early = jnp.concatenate([mm_tn(tokens, gate_low).astype(BF), mm_tn(cot_all, hidden).astype(BF)], axis=1)
    early = scatter_dp(early)
    low, conv_sum, head_sum, skip_sum = backward(
        keep, act, pre, z, cum, sin, dy, conv, head, chan, ones, tri, heads
    )
    lows = jnp.concatenate([gate_low, low], axis=1)
    normed_grad = scatter_tensor(mm_nt(lows, full_in).astype(BF))
    late_sums = scatter_dp(mm_tn(tokens, low).astype(BF))

    projected = jnp.sum(normed_grad * in_gain * resid, axis=-1, keepdims=True) / d
    x_grad = inverse * in_gain * normed_grad - resid * inverse**3 * projected + cotangent.astype(F32)

    w_z_grad, w_out_grad = early[:, :width], early[:, width:]
    w_x_grad, bc_part, dt_part = late_sums[:, :width], late_sums[:, width:cols], late_sums[:, cols:]
    dots = (
        jnp.sum(w_z.astype(F32) * w_z_grad, axis=1)
        + jnp.sum(w_x.astype(F32) * w_x_grad, axis=1)
        + jnp.sum(w_dt.astype(F32) * dt_part[:, :heads], axis=1)
    )
    pack = jnp.concatenate([bc_part, jnp.broadcast_to(dots[:, None], (own, 128))], axis=1)
    pack = total(pack, "tensor", (YS, ZN, ZF))
    w_bc_grad = pack[:, : 2 * NS]
    dots = pack[:, 2 * NS] + jnp.sum(w_bc.astype(F32) * w_bc_grad, axis=1)
    each = own // 8
    gain = lax.dynamic_slice_in_dim(in_gain, dp * own + t * each, each, 0)
    in_gain_grad = lax.dynamic_slice_in_dim(dots, t * each, each, 0) / gain

    small = jnp.concatenate(
        [
            conv_sum[:5],
            jnp.concatenate([gain_sum[:1], head_sum[:1], head_sum[1:2]], axis=1),
            jnp.pad(skip_sum[:1], ((0, 0), (0, 2 * NS))),
            jnp.zeros((1, cols), F32),
        ]
    )
    small = total(small, "dp", (CS, XN, XF, YL))
    bc_small = total(small[:, width:], "tensor", (YS, ZN, ZF))
    return (
        output,
        x_grad,
        in_gain_grad,
        w_z_grad,
        w_x_grad,
        dt_part[:, :heads],
        w_bc_grad,
        small[:4, :width],
        small[4, :width],
        bc_small[:4],
        bc_small[4],
        small[5, width : width + heads],
        small[5, width + 128 : width + 128 + heads],
        jnp.sum(small[6, :width].reshape(heads, HD), axis=1),
        small[5, :width],
        w_out_grad,
    )


def solution(mesh):
    placed = (
        P(("dp", "tensor"), None),
        P(("dp", "tensor"), None),
        P("dp", None),
        P(),
        P("dp", "tensor"),
        P("dp", "tensor"),
        P("dp", "tensor"),
        P("dp", None),
        P(None, "tensor"),
        P("tensor"),
        P(),
        P(),
        P("tensor"),
        P("tensor"),
        P("tensor"),
        P("tensor"),
        P("dp", "tensor"),
    )
    return jax.shard_map(
        local,
        mesh=mesh,
        in_specs=placed,
        out_specs=(
            P(("dp", "tensor"), None),
            P(("dp", "tensor"), None),
            P(("dp", "tensor")),
            P("dp", "tensor"),
            P("dp", "tensor"),
            P("dp", "tensor"),
            P("dp", None),
            P(None, "tensor"),
            P("tensor"),
            P(),
            P(),
            P("tensor"),
            P("tensor"),
            P("tensor"),
            P("tensor"),
            P("dp", "tensor"),
        ),
        check_vma=False,
    )
```

time: 1460 us -> 531 us (0.36)
  waiting for transfers between devices: 523 us -> 215 us
  local copies, waits for them, and re-layouts: 272 us -> 41.8 us
  matrix products: 261 us -> 33.3 us
  blocking collectives: 210 us -> 0 us
  other arithmetic: 163 us -> 42.7 us
  starting transfers between devices: 1.31 us -> 96.2 us
  Pallas kernels: 0 us -> 76.7 us
    reduce_scatter x6 -> x0, waiting for transfers between devices: 381 us -> none  [the longest x1 98.9 us: local(): lax.psum_scatter(running + contract_cols(step_low, back_dt), 'tensor', sc...]
    dot_general x126 -> x5, matrix products: 256 us -> 33.3 us  [the longest x3 19.7 us: mm_tn(): lax.dot_general(a, b, (((0,), (0,)), ((), ())), preferred_element_type=F32)]
    ppermute x0 -> x71, waiting for transfers between devices: none -> 215 us  [the longest x26 89.8 us: gather_tensor(): send = lambda v, to: lax.ppermute(v, 'tensor', to)]
    dynamic_update_slice x40 -> x3, local copies, waits for them, and re-layouts: 164 us -> 3.76 us  [put(): return lax.dynamic_update_slice_in_dim(out, piece, at, 0)]
    psum x3 -> x0, blocking collectives: 97.7 us -> none  [the longest x1 54 us: local(): lax.psum((taps_x_grad, offset_x_grad, taps_bc_grad, offset_bc_grad, bias_...]
    ppermute x0 -> x71, starting transfers between devices: none -> 96.1 us  [the longest x26 37 us: gather_tensor(): send = lambda v, to: lax.ppermute(v, 'tensor', to)]
    another operation x67 -> x19, other arithmetic: 97.1 us -> 3.16 us  [the longest x12 2.68 us: ring_sum(): ahead = jnp.stack([(up(ahead[0]) + up(from_left)).astype(BF), ahead[1]])]
    pallas_call x0 -> x4, Pallas kernels: none -> 76.7 us  [the longest x1 31.5 us: backward(): pl.pallas_call(functools.partial(backward_kernel, heads=heads, count=n),...]
  transfers between devices with their start and end apart: 13 -> 72, of which waited for: 10 -> 39; matrix products, arithmetic and copies ran while one was open for 23% -> 16% of each run, Pallas kernels for 0% -> 0%
where the time goes in v1:
time: 531 us; the launch traced here: 521 us
  waiting for transfers between devices  215 us (40%)
  starting transfers between devices  96.2 us (18%)
  Pallas kernels  76.7 us (14%)
  other arithmetic  42.7 us (8%)
  local copies, waits for them, and re-layouts  41.8 us (8%)
  matrix products  33.3 us (6%)
  between operations  15.8 us (3%)
    ppermute x26, waiting for transfers between devices, gather_tensor(): send = lambda v, to: lax.ppermute(v, 'tensor', to)  89.8 us
    ppermute x20, waiting for transfers between devices, scatter_tensor(): send = lambda v, to: lax.ppermute(v, 'tensor', to)  56 us
    ppermute x13, waiting for transfers between devices, total(): value = value + lax.ppermute(value, axis, to)  40.7 us
    ppermute x26, starting transfers between devices, gather_tensor(): send = lambda v, to: lax.ppermute(v, 'tensor', to)  37 us
    ppermute x20, starting transfers between devices, scatter_tensor(): send = lambda v, to: lax.ppermute(v, 'tensor', to)  32.9 us
    pallas_call x1, Pallas kernels, backward(): pl.pallas_call(functools.partial(backward_kernel, heads=heads, count=n),...  31.5 us
    ppermute x12, waiting for transfers between devices, scatter_dp(): send = lambda v, to: lax.ppermute(v, 'dp', to)  28.5 us
    pallas_call x1, Pallas kernels, forward(): pl.pallas_call(functools.partial(forward_kernel, heads=heads), grid_spec=...  22.1 us
  transfers between devices with their start and end apart: 72, of which 39 were waited for; matrix products, arithmetic and copies ran while one was open for 16% of the time, Pallas kernels for 0%

profile of v1, /device:TPU:0, one launch (start us, length us, event | category | flops | bytes accessed | tf_op | source)
XLA Modules:
  0.0 521.3 jit_solution(5129255064925447405)
XLA Ops:
  15.6 4.2 collective-permute-start.15
  52.5 5.2 %collective-permute-done.9 = bf16[48,1536]{1,0:T(8,128)(2,1)S(1)} collective-permute-done((bf16[48,1536]{1,0:T(8,128)(2,1)S(1)}, bf16[48,1536]{1,0:T(8,128)(2,1)S(1)}, u32[]{:S(2)}, u32[]{:S(2)}) %collective-permute-start.9) | collective-permute-done | bytes 147488 | tf_op jit(solution)/shard_map/ppermute | solution.py:467
  60.1 8.9 %collective-permute-done = bf16[160,1536]{1,0:T(8,128)(2,1)S(1)} collective-permute-done((bf16[160,1536]{1,0:T(8,128)(2,1)}, bf16[160,1536]{1,0:T(8,128)(2,1)S(1)}, u32[]{:S(2)}, u32[]{:S(2)}) %collective-permute-start) | collective-permute-done | bytes 491552 | tf_op jit(solution)/shard_map/ppermute | solution.py:467
  70.7 17.2 %collective-permute-done.16 = bf16[288,1536]{1,0:T(8,128)(2,1)S(1)} collective-permute-done((bf16[288,1536]{1,0:T(8,128)(2,1)S(1)}, bf16[288,1536]{1,0:T(8,128)(2,1)S(1)}, u32[]{:S(2)}, u32[]{:S(2)}) %collective-permute-start.16) | collective-permute-done | bytes 884768 | tf_op jit(solution)/shard_map/ppermute | solution.py:467
  91.8 14.4 %collective-permute-done.3 = bf16[288,1536]{1,0:T(8,128)(2,1)S(1)} collective-permute-done((bf16[288,1536]{1,0:T(8,128)(2,1)S(1)}, bf16[288,1536]{1,0:T(8,128)(2,1)S(1)}, u32[]{:S(2)}, u32[]{:S(2)}) %collective-permute-start.3) | collective-permute-done | bytes 884768 | tf_op jit(solution)/shard_map/ppermute | solution.py:467
  117.6 9.5 %collective-permute-done.19 = bf16[160,1536]{1,0:T(8,128)(2,1)S(1)} collective-permute-done((bf16[160,1536]{1,0:T(8,128)(2,1)}, bf16[160,1536]{1,0:T(8,128)(2,1)S(1)}, u32[]{:S(2)}, u32[]{:S(2)}) %collective-permute-start.19) | collective-permute-done | bytes 491552 | tf_op jit(solution)/shard_map/ppermute | solution.py:467
  128.0 9.6 %collective-permute-done.6 = bf16[160,1536]{1,0:T(8,128)(2,1)S(1)} collective-permute-done((bf16[160,1536]{1,0:T(8,128)(2,1)S(1)}, bf16[160,1536]{1,0:T(8,128)(2,1)S(1)}, u32[]{:S(2)}, u32[]{:S(2)}) %collective-permute-start.6) | collective-permute-done | bytes 491552 | tf_op jit(solution)/shard_map/ppermute | solution.py:467
  141.6 7.1 %collective-permute-done.7 = bf16[160,1536]{1,0:T(8,128)(2,1)S(1)} collective-permute-done((bf16[160,1536]{1,0:T(8,128)(2,1)S(1)}, bf16[160,1536]{1,0:T(8,128)(2,1)S(1)}, u32[]{:S(2)}, u32[]{:S(2)}) %collective-permute-start.7) | collective-permute-done | bytes 491552 | tf_op jit(solution)/shard_map/ppermute | solution.py:467
  157.4 4.9 collective-permute-done.24
  163.2 4.3 collective-permute-done.11
  168.5 22.1 %ssd_forward.1 = (f32[2048,384]{1,0:T(8,128)}, f32[2048,640]{1,0:T(8,128)}, bf16[2048,640]{1,0:T(8,128)(2,1)}, f32[2048,128]{1,0:T(8,128)}, f32[2048,128]{1,0:T(...) custom-call(s32[9]{0:T(128)} %get-tuple-element.101.keep_ref, ...), custom_call_target="tpu_custom_call" | custom-call | flops 12000000000 | bytes 30000000 | tf_op jit(solution)/shard_map/ssd_forward/pallas_call | solution.py:159
  190.6 11.9 %grad_sums.1 = (f32[2048,384]{1,0:T(8,128)}, f32[8,2048]{1,0:T(8,128)}) custom-call(s32[9]{0:T(128)} %get-tuple-element.102.live_ref, bf16[2048,1536]{1,0:T(8,128)(2,1)} %maximum_dynamic-update-slice_fusion.5.cot_ref, bf16[1536,1536]{1,0:T(8,128)(2,1)} %all-gather.2.cloned.1.call-done.w_ref, f32[2048,384]{1,0:T(8,128)} %get-tuple-element.33.mixed_ref, ...), custom_call_target="tpu_custom_call" | custom-call | flops 2415919104 | bytes 17000000 | tf_op jit(solution)/shard_map/grad_sums/pallas_call | solution.py:210
  203.5 5.0 collective-permute-done.26
  220.2 11.3 %gate_back.1 = (bf16[2048,384]{1,0:T(8,128)(2,1)}, bf16[2048,384]{1,0:T(8,128)(2,1)}, f32[2048,384]{1,0:T(8,128)}, f32[8,384]{1,0:T(8,128)}) custom-call(s32[9]{0:T(128)} %get-tuple-element.102.live_ref, f32[2048,384]{1,0:T(8,128)} %get-tuple-element.35.hg_ref, f32[2048,384]{1,0:T(8,128)} %get-tuple-element.33.mixed_ref, ...), custom_call_target="tpu_custom_call" | custom-call | flops 15728640 | bytes 16000000 | tf_op jit(solution)/shard_map/gate_back/pallas_call | solution.py:266
  231.5 31.5 %ssd_backward.1 = (bf16[2048,768]{1,0:T(8,128)(2,1)}, f32[8,640]{1,0:T(8,128)}, f32[8,128]{1,0:T(8,128)}, f32[8,384]{1,0:T(8,128)}) custom-call(s32[9]{0:T(128)} %get-tuple-element.101.keep_ref, bf16[2048,640]{1,0:T(8,128)(2,1)} %get-tuple-element.39.act_ref, f32[2048,640]{1,0:T(8,128)} %get-tuple-element.40.pre_ref.before_ref, ...), custom_call_target="tpu_custom_call" | custom-call | flops 30000001024 | bytes 25000000 | tf_op jit(solution)/shard_map/ssd_backward/pallas_call | solution.py:412
  263.0 10.0 %convolution_convert_fusion = bf16[2048,1536]{1,0:T(8,128)(2,1)S(1)} fusion(bf16[2048,768]{1,0:T(8,128)(2,1)} %get-tuple-element.45, bf16[2048,384]{1,0:T(8,128)(2,1)S(1)} %copy-done.37, bf16[1536,1536]{1,0:T(8,128)(2,1)S(1)} %bitcast.253), kind=kOutput, calls=%fused_computation | convolution fusion | flops 7260340224 | bytes 14548992 | tf_op jit(solution)/shard_map/dot_general | solution.py:24
  275.0 8.8 %convolution_convert_fusion.2 = bf16[1536,768]{1,0:T(8,128)(2,1)S(1)} fusion(bf16[2048,1536]{1,0:T(8,128)(2,1)} %maximum_dynamic-update-slice_fusion.11.tok_ref, bf16[2048,768]{1,0:T(8,128)(2,1)S(1)} %copy-done.40), kind=kOutput, calls=%fused_computation.6 | convolution fusion | flops 4833017856 | bytes 11796480 | tf_op jit(solution)/shard_map/dot_general | solution.py:28
  283.8 5.4 %convolution_convert_fusion.4 = bf16[1536,384]{0,1:T(8,128)(2,1)S(1)} fusion(bf16[2048,1536]{1,0:T(8,128)(2,1)} %maximum_dynamic-update-slice_fusion.11.tok_ref, bf16[2048,384]{1,0:T(8,128)(2,1)S(1)} %copy-done.38), kind=kOutput, calls=%fused_computation.13 | convolution fusion | flops 2416508928 | bytes 9043968 | tf_op jit(solution)/shard_map/dot_general | solution.py:28
  291.5 5.4 %convolution_convert_fusion.3 = bf16[1536,384]{0,1:T(8,128)(2,1)S(1)} fusion(bf16[2048,1536]{1,0:T(8,128)(2,1)} %maximum_dynamic-update-slice_fusion.5.cot_ref, bf16[2048,384]{1,0:T(8,128)(2,1)S(1)} %copy-done.36), kind=kOutput, calls=%fused_computation.12 | convolution fusion | flops 2416508928 | bytes 9043968 | tf_op jit(solution)/shard_map/dot_general | solution.py:28
  300.8 3.7 convolution_convert_fusion.1
  313.5 4.2 collective-permute-start.66
  321.6 4.3 copy.57
  325.9 14.5 %collective-permute-done.67 = f32[8,640]{1,0:T(8,128)S(1)} collective-permute-done((f32[8,640]{1,0:T(8,128)S(1)}, f32[8,640]{1,0:T(8,128)S(1)}, u32[]{:S(2)}, u32[]{:S(2)}) %collective-permute-start.67) | collective-permute-done | bytes 20512 | tf_op jit(solution)/shard_map/ppermute | solution.py:536
  361.7 4.8 collective-permute-done.29
  382.2 14.3 %collective-permute-done.45 = bf16[48,1536]{1,0:T(8,128)(2,1)S(1)} collective-permute-done((bf16[48,1536]{1,0:T(8,128)(2,1)S(1)}, bf16[48,1536]{1,0:T(8,128)(2,1)S(1)}, u32[]{:S(2)}, u32[]{:S(2)}) %collective-permute-start.45) | collective-permute-done | bytes 147488 | tf_op jit(solution)/shard_map/ppermute | solution.py:511
  396.5 18.4 %collective-permute-done.47 = bf16[48,1536]{1,0:T(8,128)(2,1)S(1)} collective-permute-done((bf16[48,1536]{1,0:T(8,128)(2,1)S(1)}, bf16[48,1536]{1,0:T(8,128)(2,1)S(1)}, u32[]{:S(2)}, u32[]{:S(2)}) %collective-permute-start.47) | collective-permute-done | bytes 147488 | tf_op jit(solution)/shard_map/ppermute | solution.py:511
  439.8 15.5 %collective-permute-done.30 = bf16[2,160,1536]{2,1,0:T(8,128)(2,1)S(1)} collective-permute-done((bf16[2,160,1536]{2,1,0:T(8,128)(2,1)S(1)}, bf16[2,160,1536]{2,1,0:T(8,128)(2,1)S(1)}, u32[]{:S(2)}, u32[]{:S(2)}) %collective-permute-start.30) | collective-permute-done | bytes 983072 | tf_op jit(solution)/shard_map/ppermute | solution.py:511
  462.0 4.0 collective-permute-done.51
  470.6 15.4 %collective-permute-done.54 = bf16[96,768]{1,0:T(8,128)(2,1)S(1)} collective-permute-done((bf16[96,768]{1,0:T(8,128)(2,1)S(1)}, bf16[96,768]{1,0:T(8,128)(2,1)S(1)}, u32[]{:S(2)}, u32[]{:S(2)}) %collective-permute-start.54) | collective-permute-done | bytes 147488 | tf_op jit(solution)/shard_map/ppermute | solution.py:526
  487.4 3.7 collective-permute-done.60
  495.8 3.9 collective-permute-done.61
  508.7 3.9 collective-permute-done.63
  (366 shorter events, 198.5 us)
Async XLA Ops:
  7.2 161.4 %all-gather.2.cloned.1.call-start = ((), (), s32[]{:S(2)}) async-start(), calls=%async_computation | async-start | bytes 5013504 | tf_op jit(solution)/shard_map/all_gather | solution.py:584
  15.6 20.9 %collective-permute-start.15 = (bf16[96,1536]{1,0:T(8,128)(2,1)S(1)}, bf16[96,1536]{1,0:T(8,128)(2,1)S(1)}, u32[]{:S(2)}, u32[]{:S(2)}) collective-permute-start(bf16[96,1536]{1,0:T(8,128)(2,1)S(1)} %slice.392), channel_id=1, source_target_pairs={{0,6},{1,7},{2,0},{3,1},{4,2},{5,3},{6,4},{7,5},{8,14},{9,15},{10,... | collective-permute-start | bytes 884744 | tf_op jit(solution)/shard_map/ppermute | solution.py:467
  19.8 20.4 %collective-permute-start.2 = (bf16[96,1536]{1,0:T(8,128)(2,1)S(1)}, bf16[96,1536]{1,0:T(8,128)(2,1)S(1)}, u32[]{:S(2)}, u32[]{:S(2)}) collective-permute-start(bf16[96,1536]{1,0:T(8,128)(2,1)S(1)} %slice.385), channel_id=1, source_target_pairs={{0,6},{1,7},{2,0},{3,1},{4,2},{5,3},{6,4},{7,5},{8,14},{9,15},{10,... | collective-permute-start | bytes 884744 | tf_op jit(solution)/shard_map/ppermute | solution.py:467
  24.0 33.8 %collective-permute-start.13 = (bf16[160,1536]{1,0:T(8,128)(2,1)}, bf16[160,1536]{1,0:T(8,128)(2,1)}, u32[]{:S(2)}, u32[]{:S(2)}) collective-permute-start(bf16[160,1536]{1,0:T(8,128)(2,1)} %slice.391), channel_id=1, source_target_pairs={{0,1},{1,0},{2,3},{3,2},{4,5},{5,4},{6,7},{7,6},{8,9},{9,8},{10,11... | collective-permute-start | bytes 1474568 | tf_op jit(solution)/shard_map/ppermute | solution.py:467
  36.5 32.5 %collective-permute-start = (bf16[160,1536]{1,0:T(8,128)(2,1)}, bf16[160,1536]{1,0:T(8,128)(2,1)S(1)}, u32[]{:S(2)}, u32[]{:S(2)}) collective-permute-start(bf16[160,1536]{1,0:T(8,128)(2,1)} %slice.384), channel_id=1, source_target_pairs={{0,1},{1,0},{2,3},{3,2},{4,5},{5,4},{6,7},{7,6},{8,9},{9,8},{10,11... | collective-permute-start | bytes 1474568 | tf_op jit(solution)/shard_map/ppermute | solution.py:467
  36.9 51.0 %collective-permute-start.16 = (bf16[288,1536]{1,0:T(8,128)(2,1)S(1)}, bf16[288,1536]{1,0:T(8,128)(2,1)S(1)}, u32[]{:S(2)}, u32[]{:S(2)}) collective-permute-start(bf16[288,1536]{1,0:T(8,128)(2,1)S(1)} %pad_maximum_fusion.7), channel_id=1, source_target_pairs={{0,1},{1,0},{2,3},{3,2},{4,5},{5,4},{6,7},{7,6},{8,9},{9,8},{10,11... | collective-permute-start | bytes 2654216 | tf_op jit(solution)/shard_map/ppermute | solution.py:467
  52.5 55.7 %collective-permute-start.17 = (bf16[160,1536]{1,0:T(8,128)(2,1)}, bf16[160,1536]{1,0:T(8,128)(2,1)S(1)}, u32[]{:S(2)}, u32[]{:S(2)}) collective-permute-start(bf16[160,1536]{1,0:T(8,128)(2,1)} %slice.391), channel_id=1, source_target_pairs={{0,2},{1,3},{2,4},{3,5},{4,6},{5,7},{6,0},{7,1},{8,10},{9,11},{10,... | collective-permute-start | bytes 1474568 | tf_op jit(solution)/shard_map/ppermute | solution.py:467
  57.8 55.9 %collective-permute-start.18 = (bf16[160,1536]{1,0:T(8,128)(2,1)}, bf16[160,1536]{1,0:T(8,128)(2,1)S(1)}, u32[]{:S(2)}, u32[]{:S(2)}) collective-permute-start(bf16[160,1536]{1,0:T(8,128)(2,1)} %slice.391), channel_id=1, source_target_pairs={{0,6},{1,7},{2,0},{3,1},{4,2},{5,3},{6,4},{7,5},{8,14},{9,15},{10,... | collective-permute-start | bytes 1474568 | tf_op jit(solution)/shard_map/ppermute | solution.py:467
  57.8 48.4 %collective-permute-start.3 = (bf16[288,1536]{1,0:T(8,128)(2,1)S(1)}, bf16[288,1536]{1,0:T(8,128)(2,1)S(1)}, u32[]{:S(2)}, u32[]{:S(2)}) collective-permute-start(bf16[288,1536]{1,0:T(8,128)(2,1)S(1)} %pad_maximum_fusion.6), channel_id=1, source_target_pairs={{0,1},{1,0},{2,3},{3,2},{4,5},{5,4},{6,7},{7,6},{8,9},{9,8},{10,11... | collective-permute-start | bytes 2654216 | tf_op jit(solution)/shard_map/ppermute | solution.py:467
  69.0 42.5 %collective-permute-start.4 = (bf16[160,1536]{1,0:T(8,128)(2,1)S(1)}, bf16[160,1536]{1,0:T(8,128)(2,1)S(1)}, u32[]{:S(2)}, u32[]{:S(2)}) collective-permute-start(bf16[160,1536]{1,0:T(8,128)(2,1)S(1)} %copy-done.19), channel_id=1, source_target_pairs={{0,2},{1,3},{2,4},{3,5},{4,6},{5,7},{6,0},{7,1},{8,10},{9,11},{10,... | collective-permute-start | bytes 1474568 | tf_op jit(solution)/shard_map/ppermute | solution.py:467
  87.9 28.7 %collective-permute-start.5 = (bf16[160,1536]{1,0:T(8,128)(2,1)S(1)}, bf16[160,1536]{1,0:T(8,128)(2,1)S(1)}, u32[]{:S(2)}, u32[]{:S(2)}) collective-permute-start(bf16[160,1536]{1,0:T(8,128)(2,1)S(1)} %copy-done.19), channel_id=1, source_target_pairs={{0,6},{1,7},{2,0},{3,1},{4,2},{5,3},{6,4},{7,5},{8,14},{9,15},{10,... | collective-permute-start | bytes 1474568 | tf_op jit(solution)/shard_map/ppermute | solution.py:467
  106.2 51.2 %collective-permute-start.25 = (bf16[96,1536]{1,0:T(8,128)(2,1)S(1)}, bf16[96,1536]{1,0:T(8,128)(2,1)S(1)}, u32[]{:S(2)}, u32[]{:S(2)}) collective-permute-start(bf16[96,1536]{1,0:T(8,128)(2,1)S(1)} %pad_maximum_fusion.9), channel_id=1, source_target_pairs={{0,1},{1,0},{2,3},{3,2},{4,5},{5,4},{6,7},{7,6},{8,9},{9,8},{10,11... | collective-permute-start | bytes 884744 | tf_op jit(solution)/shard_map/ppermute | solution.py:467
  108.2 55.1 %collective-permute-start.12 = (bf16[96,1536]{1,0:T(8,128)(2,1)S(1)}, bf16[96,1536]{1,0:T(8,128)(2,1)S(1)}, u32[]{:S(2)}, u32[]{:S(2)}) collective-permute-start(bf16[96,1536]{1,0:T(8,128)(2,1)S(1)} %pad_maximum_fusion.8), channel_id=1, source_target_pairs={{0,1},{1,0},{2,3},{3,2},{4,5},{5,4},{6,7},{7,6},{8,9},{9,8},{10,11... | collective-permute-start | bytes 884744 | tf_op jit(solution)/shard_map/ppermute | solution.py:467
  113.7 26.6 %collective-permute-start.20 = (bf16[160,1536]{1,0:T(8,128)(2,1)}, bf16[160,1536]{1,0:T(8,128)(2,1)S(1)}, u32[]{:S(2)}, u32[]{:S(2)}) collective-permute-start(bf16[160,1536]{1,0:T(8,128)(2,1)} %collective-permute-done.13), channel_id=1, source_target_pairs={{0,6},{1,7},{2,0},{3,1},{4,2},{5,3},{6,4},{7,5},{8,14},{9,15},{10,... | collective-permute-start | bytes 1474568 | tf_op jit(solution)/shard_map/ppermute | solution.py:467
  116.6 21.0 %collective-permute-start.6 = (bf16[160,1536]{1,0:T(8,128)(2,1)S(1)}, bf16[160,1536]{1,0:T(8,128)(2,1)S(1)}, u32[]{:S(2)}, u32[]{:S(2)}) collective-permute-start(bf16[160,1536]{1,0:T(8,128)(2,1)S(1)} %collective-permute-done), channel_id=1, source_target_pairs={{0,2},{1,3},{2,4},{3,5},{4,6},{5,7},{6,0},{7,1},{8,10},{9,11},{10,... | collective-permute-start | bytes 1474568 | tf_op jit(solution)/shard_map/ppermute | solution.py:467
  127.1 24.9 %collective-permute-start.21 = (bf16[160,1536]{1,0:T(8,128)(2,1)S(1)}, bf16[160,1536]{1,0:T(8,128)(2,1)S(1)}, u32[]{:S(2)}, u32[]{:S(2)}) collective-permute-start(bf16[160,1536]{1,0:T(8,128)(2,1)S(1)} %collective-permute-done.17), channel_id=1, source_target_pairs={{0,2},{1,3},{2,4},{3,5},{4,6},{5,7},{6,0},{7,1},{8,10},{9,11},{10,... | collective-permute-start | bytes 1474568 | tf_op jit(solution)/shard_map/ppermute | solution.py:467
  290.3 80.8 %collective-permute-start.44 = (bf16[4,96,1536]{2,1,0:T(8,128)(2,1)}, bf16[4,96,1536]{2,1,0:T(8,128)(2,1)}, u32[]{:S(2)}, u32[]{:S(2)}) collective-permute-start(bf16[4,96,1536]{2,1,0:T(8,128)(2,1)} %dynamic-slice_bitcast_fusion.1), channel_id=1, source_target_pairs={{0,1},{1,0},{2,3},{3,2},{4,5},{5,4},{6,7},{7,6},{8,9},{9,8},{10,11... | collective-permute-start | bytes 3538952 | tf_op jit(solution)/shard_map/ppermute | solution.py:511
  306.3 50.1 %collective-permute-start.39 = (bf16[160,1536]{1,0:T(8,128)(2,1)}, bf16[160,1536]{1,0:T(8,128)(2,1)}, u32[]{:S(2)}, u32[]{:S(2)}) collective-permute-start(bf16[160,1536]{1,0:T(8,128)(2,1)} %get-tuple-element.115), channel_id=1, source_target_pairs={{0,2},{1,3},{2,4},{3,5},{4,6},{5,7},{6,0},{7,1},{8,10},{9,11},{10,... | collective-permute-start | bytes 1474568 | tf_op jit(solution)/shard_map/ppermute | solution.py:511
  306.6 53.0 %collective-permute-start.41 = (bf16[160,1536]{1,0:T(8,128)(2,1)}, bf16[160,1536]{1,0:T(8,128)(2,1)}, u32[]{:S(2)}, u32[]{:S(2)}) collective-permute-start(bf16[160,1536]{1,0:T(8,128)(2,1)} %get-tuple-element.117), channel_id=1, source_target_pairs={{0,6},{1,7},{2,0},{3,1},{4,2},{5,3},{6,4},{7,5},{8,14},{9,15},{10,... | collective-permute-start | bytes 1474568 | tf_op jit(solution)/shard_map/ppermute | solution.py:511
  310.9 62.3 %collective-permute-start.34 = (bf16[4,96,1536]{2,1,0:T(8,128)(2,1)}, bf16[4,96,1536]{2,1,0:T(8,128)(2,1)}, u32[]{:S(2)}, u32[]{:S(2)}) collective-permute-start(bf16[4,96,1536]{2,1,0:T(8,128)(2,1)} %dynamic-slice_bitcast_fusion.2), channel_id=1, source_target_pairs={{0,1},{1,0},{2,3},{3,2},{4,5},{5,4},{6,7},{7,6},{8,9},{9,8},{10,11... | collective-permute-start | bytes 3538952 | tf_op jit(solution)/shard_map/ppermute | solution.py:511
  319.4 21.0 %collective-permute-start.67 = (f32[8,640]{1,0:T(8,128)S(1)}, f32[8,640]{1,0:T(8,128)S(1)}, u32[]{:S(2)}, u32[]{:S(2)}) collective-permute-start(f32[8,640]{1,0:T(8,128)S(1)} %add.658), channel_id=1, source_target_pairs={{0,64},{8,72},{16,80},{24,88},{32,96},{40,104},{48,112},{56,120},{... | collective-permute-start | bytes 61448 | tf_op jit(solution)/shard_map/ppermute | solution.py:536
  367.0 67.7 %collective-permute-start.42 = (bf16[2,160,1536]{2,1,0:T(8,128)(2,1)S(1)}, bf16[2,160,1536]{2,1,0:T(8,128)(2,1)S(1)}, u32[]{:S(2)}, u32[]{:S(2)}) collective-permute-start(bf16[2,160,1536]{2,1,0:T(8,128)(2,1)S(1)} %pad_maximum_fusion.5), channel_id=1, source_target_pairs={{0,6},{1,7},{2,0},{3,1},{4,2},{5,3},{6,4},{7,5},{8,14},{9,15},{10,... | collective-permute-start | bytes 2949128 | tf_op jit(solution)/shard_map/ppermute | solution.py:511
  371.1 63.8 %collective-permute-start.40 = (bf16[2,160,1536]{2,1,0:T(8,128)(2,1)S(1)}, bf16[2,160,1536]{2,1,0:T(8,128)(2,1)S(1)}, u32[]{:S(2)}, u32[]{:S(2)}) collective-permute-start(bf16[2,160,1536]{2,1,0:T(8,128)(2,1)S(1)} %pad_maximum_fusion.4), channel_id=1, source_target_pairs={{0,2},{1,3},{2,4},{3,5},{4,6},{5,7},{6,0},{7,1},{8,10},{9,11},{10,... | collective-permute-start | bytes 2949128 | tf_op jit(solution)/shard_map/ppermute | solution.py:511
  373.2 66.4 %collective-permute-start.32 = (bf16[2,160,1536]{2,1,0:T(8,128)(2,1)S(1)}, bf16[2,160,1536]{2,1,0:T(8,128)(2,1)S(1)}, u32[]{:S(2)}, u32[]{:S(2)}) collective-permute-start(bf16[2,160,1536]{2,1,0:T(8,128)(2,1)S(1)} %pad_maximum_fusion.3), channel_id=1, source_target_pairs={{0,6},{1,7},{2,0},{3,1},{4,2},{5,3},{6,4},{7,5},{8,14},{9,15},{10,... | collective-permute-start | bytes 2949128 | tf_op jit(solution)/shard_map/ppermute | solution.py:511
  378.4 36.5 %collective-permute-start.47 = (bf16[48,1536]{1,0:T(8,128)(2,1)S(1)}, bf16[48,1536]{1,0:T(8,128)(2,1)S(1)}, u32[]{:S(2)}, u32[]{:S(2)}) collective-permute-start(bf16[48,1536]{1,0:T(8,128)(2,1)S(1)} %get-tuple-element.143), channel_id=1, source_target_pairs={{0,6},{1,7},{2,0},{3,1},{4,2},{5,3},{6,4},{7,5},{8,14},{9,15},{10,... | collective-permute-start | bytes 442376 | tf_op jit(solution)/shard_map/ppermute | solution.py:511
  429.3 25.9 %collective-permute-start.30 = (bf16[2,160,1536]{2,1,0:T(8,128)(2,1)S(1)}, bf16[2,160,1536]{2,1,0:T(8,128)(2,1)S(1)}, u32[]{:S(2)}, u32[]{:S(2)}) collective-permute-start(bf16[2,160,1536]{2,1,0:T(8,128)(2,1)S(1)} %pad_maximum_fusion.2), channel_id=1, source_target_pairs={{0,2},{1,3},{2,4},{3,5},{4,6},{5,7},{6,0},{7,1},{8,10},{9,11},{10,... | collective-permute-start | bytes 2949128 | tf_op jit(solution)/shard_map/ppermute | solution.py:511
  431.3 26.8 %collective-permute-start.48 = (bf16[2,48,1536]{2,1,0:T(8,128)(2,1)S(1)}, bf16[2,48,1536]{2,1,0:T(8,128)(2,1)S(1)}, u32[]{:S(2)}, u32[]{:S(2)}) collective-permute-start(bf16[2,48,1536]{2,1,0:T(8,128)(2,1)S(1)} %pad_maximum_fusion.13), channel_id=1, source_target_pairs={{0,6},{1,7},{2,0},{3,1},{4,2},{5,3},{6,4},{7,5},{8,14},{9,15},{10,... | collective-permute-start | bytes 884744 | tf_op jit(solution)/shard_map/ppermute | solution.py:511
  434.8 25.0 %collective-permute-start.46 = (bf16[2,48,1536]{2,1,0:T(8,128)(2,1)S(1)}, bf16[2,48,1536]{2,1,0:T(8,128)(2,1)S(1)}, u32[]{:S(2)}, u32[]{:S(2)}) collective-permute-start(bf16[2,48,1536]{2,1,0:T(8,128)(2,1)S(1)} %pad_maximum_fusion.12), channel_id=1, source_target_pairs={{0,2},{1,3},{2,4},{3,5},{4,6},{5,7},{6,0},{7,1},{8,10},{9,11},{10,... | collective-permute-start | bytes 884744 | tf_op jit(solution)/shard_map/ppermute | solution.py:511
  434.9 59.3 %collective-permute-start.38 = (bf16[2,48,1536]{2,1,0:T(8,128)(2,1)S(1)}, bf16[2,48,1536]{2,1,0:T(8,128)(2,1)S(1)}, u32[]{:S(2)}, u32[]{:S(2)}) collective-permute-start(bf16[2,48,1536]{2,1,0:T(8,128)(2,1)S(1)} %pad_maximum_fusion.11), channel_id=1, source_target_pairs={{0,6},{1,7},{2,0},{3,1},{4,2},{5,3},{6,4},{7,5},{8,14},{9,15},{10,... | collective-permute-start | bytes 884744 | tf_op jit(solution)/shard_map/ppermute | solution.py:511
  439.7 54.5 %collective-permute-start.36 = (bf16[2,48,1536]{2,1,0:T(8,128)(2,1)S(1)}, bf16[2,48,1536]{2,1,0:T(8,128)(2,1)S(1)}, u32[]{:S(2)}, u32[]{:S(2)}) collective-permute-start(bf16[2,48,1536]{2,1,0:T(8,128)(2,1)S(1)} %pad_maximum_fusion.10), channel_id=1, source_target_pairs={{0,2},{1,3},{2,4},{3,5},{4,6},{5,7},{6,0},{7,1},{8,10},{9,11},{10,... | collective-permute-start | bytes 884744 | tf_op jit(solution)/shard_map/ppermute | solution.py:511
  466.0 34.7 %collective-permute-start.43 = (bf16[160,1536]{1,0:T(8,128)(2,1)}, bf16[160,1536]{1,0:T(8,128)(2,1)}, u32[]{:S(2)}, u32[]{:S(2)}) collective-permute-start(bf16[160,1536]{1,0:T(8,128)(2,1)} %fusion.28), channel_id=1, source_target_pairs={{0,1},{1,0},{2,3},{3,2},{4,5},{5,4},{6,7},{7,6},{8,9},{9,8},{10,11... | collective-permute-start | bytes 1474568 | tf_op jit(solution)/shard_map/ppermute | solution.py:511
  467.6 34.8 %collective-permute-start.33 = (bf16[160,1536]{1,0:T(8,128)(2,1)}, bf16[160,1536]{1,0:T(8,128)(2,1)}, u32[]{:S(2)}, u32[]{:S(2)}) collective-permute-start(bf16[160,1536]{1,0:T(8,128)(2,1)} %fusion.27), channel_id=1, source_target_pairs={{0,1},{1,0},{2,3},{3,2},{4,5},{5,4},{6,7},{7,6},{8,9},{9,8},{10,11... | collective-permute-start | bytes 1474568 | tf_op jit(solution)/shard_map/ppermute | solution.py:511
  (83 other events, 905.8 us)
Sparse Core Ops, SparseCore 0:
  10.0 56.3 all-gather.1
